TPU v7x, 256 devices: a whole 4x4x8 slice. The times are simulated.
256 devices in a mesh: chan: 4 (over x_lo, core), pair: 16 (over z, x_hi), tm: 4 (over y).
Axes of the slice: x: 4 (x_hi: 2, x_lo: 2; x = x_hi * 2 + x_lo), y: 4, z: 8, core: 2. Of those that a mesh axis runs over, the one named last changes fastest.
Arguments:
- voltages: bfloat16 [16, 128, 524288], P('pair', 'chan', 'tm'), may hold values from -127 to 127, as said below
- selected: int32 [32], replicated, may hold values from 0 to 1023, as said below
Outputs:
- visibility: float32 [2, 32, 2048, 2048], P(None, 'chan', 'pair', 'tm')
Inputs may be any that keep to these rules, and one draw needn't show every extreme that they name: `voltages`: whole numbers. `selected`: 32 different channel numbers; channels 0 and 1023 are always among them.
All inputs are finite; a program needn't handle non-finite values.
Results may differ from a plain program's by a relative error of at most 0.013.
Values may be sent and summed in bfloat16 or wider, within the bound.
No kernel may reach another device: no remote copies, remote signals or barrier semaphores. Data moves between devices by JAX's collectives and lax.ppermute only.
A program may use at most 128 MiB of HBM per device.

v0:
```python
import math

import jax
import jax.numpy as jnp
from jax import lax
from jax.sharding import PartitionSpec as P

NFFT = 2048
TAPS = 4
NSEL = 32


def passed_along(block, axis, distance):
    devices = range(lax.axis_size(axis))
    route = [(i - distance, i) for i in devices if i - distance in devices]
    return lax.ppermute(block, axis, route)


def filter_taps():
    position = jnp.arange(TAPS * NFFT, dtype=jnp.float32)
    offset = (position + 0.5) / NFFT - TAPS / 2.0
    hann_part = 0.5 - 0.5 * jnp.cos(2.0 * math.pi * (position + 0.5) / (TAPS * NFFT))
    return (jnp.sinc(offset) * hann_part).reshape(TAPS, NFFT)


def transform(extended, tap_tables, frame_count):
    inputs_here = extended.shape[0]
    total = jnp.einsum(
        "isn,nq->isq",
        extended[:, 0:frame_count, :],
        tap_tables[0],
        preferred_element_type=jnp.float32,
    )
    for tap_index in range(1, TAPS):
        total = total + jnp.einsum(
            "isn,nq->isq",
            extended[:, tap_index : tap_index + frame_count, :],
            tap_tables[tap_index],
            preferred_element_type=jnp.float32,
        )
    shaped = total.reshape(inputs_here, frame_count, 2, 2, NSEL)
    joined = shaped[:, :, 0] + shaped[:, :, 1]
    return jnp.transpose(joined, (3, 0, 2, 1))


def swap_parts(columns, segments):
    shaped = columns.reshape(columns.shape[0], columns.shape[1], segments, 2, -1)
    swapped = jnp.stack([-shaped[:, :, :, 1], shaped[:, :, :, 0]], axis=3)
    return swapped.reshape(columns.shape)


def correlate(own_rows, columns, segments):
    paired = jnp.stack([columns, swap_parts(columns, segments)], axis=0)
    return jnp.einsum("cis,rcjs->rcij", own_rows, paired, preferred_element_type=jnp.float32)


def body(voltages, selected):
    local_inputs = voltages.shape[1]
    spec_dev = voltages.shape[2] // NFFT
    frames = voltages.reshape(local_inputs, spec_dev, NFFT)
    window = filter_taps()
    sample_index = jnp.arange(NFFT, dtype=jnp.int32)
    phase_index = sample_index[:, None] * selected[None, :] % NFFT
    angles = 2.0 * math.pi * phase_index.astype(jnp.float32) / NFFT
    dft_table = jnp.stack([jnp.cos(angles), -jnp.sin(angles)], axis=1)
    exact_tables = window[:, :, None, None] * dft_table[None]
    upper_part = exact_tables.astype(jnp.bfloat16)
    upper_back = lax.optimization_barrier(upper_part).astype(jnp.float32)
    lower_part = (exact_tables - upper_back).astype(jnp.bfloat16)
    tap_tables = jnp.stack([upper_part, lower_part], axis=2).reshape(TAPS, NFFT, 4 * NSEL)
    extra_frames = TAPS - 1
    rim_frames = passed_along(frames[:, spec_dev - extra_frames :, :], "tm", 1)
    spectra = transform(jnp.concatenate([rim_frames, frames], axis=1), tap_tables, spec_dev)
    factor = 1.0 / (24.0 * math.sqrt(NFFT))
    rounded = (spectra * factor).astype(jnp.bfloat16).reshape(NSEL, local_inputs, 2 * spec_dev)
    turned = lax.all_to_all(rounded, "chan", split_axis=0, concat_axis=1, tiled=True)
    inverse_count = 1.0 / (spec_dev * lax.axis_size("tm"))
    partial_sums = correlate(turned, lax.all_gather(turned, "pair", axis=1, tiled=True), 1)
    visibility = (
        lax.psum_scatter(
            partial_sums.astype(jnp.bfloat16), "tm", scatter_dimension=3, tiled=True
        ).astype(jnp.float32)
        * inverse_count
    )
    return visibility


def solution(mesh):
    return jax.shard_map(
        body,
        mesh=mesh,
        in_specs=(P("pair", "chan", "tm"), P()),
        out_specs=P(None, "chan", "pair", "tm"),
        check_vma=False,
    )
```

profile of v0, /device:TPU:2, one launch (start us, length us, event | category | flops | bytes accessed | tf_op | source)
XLA Modules:
  0.0 277.7 jit_solution(12696595899272095432)
XLA Ops:
  6.5 0.0 all-gather.2.cloned.1.call-start
  6.5 0.0 copy-start.2
  6.5 11.4 %copy.25 = bf16[4,8,64,2048]{3,2,1,0:T(8,128)(2,1)} copy(bf16[4,8,64,2048]{3,1,2,0:T(8,128)(2,1)} %bitcast.51) | data formatting | bytes 16777216
  17.9 1.5 slice.52
  19.5 3.7 %collective-permute-start = (bf16[32,3,2048]{2,1,0:T(4,128)(2,1)S(1)}, bf16[32,3,2048]{2,1,0:T(4,128)(2,1)S(1)}, u32[]{:S(2)}, u32[]{:S(2)}) collective-permute-start(bf16[32,3,2048]{2,1,0:T(4,128)(2,1)S(1)} %slice.52), channel_id=1, source_target_pairs={{0,1},{1,2},{2,3},{4,5},{5,6},{6,7},{8,9},{9,10},{10,11},{12,13},{... | collective-permute-start | bytes 1179656 | tf_op jit(solution)/shard_map/ppermute | solution.py:16
  23.2 0.3 fusion.41
  23.5 0.0 copy-done.2
  23.5 1.1 fusion.35
  24.7 0.2 multiply_convert_fusion
  24.8 0.0 copy-start
  24.8 0.2 multiply_convert_fusion.1
  25.0 0.3 fusion.22
  25.3 0.2 fusion.27
  25.5 2.7 copy-done
  28.2 2.4 convolution_bitcast_fusion
  30.6 3.5 %collective-permute-done = bf16[32,3,2048]{2,1,0:T(4,128)(2,1)S(1)} collective-permute-done((bf16[32,3,2048]{2,1,0:T(4,128)(2,1)S(1)}, bf16[32,3,2048]{2,1,0:T(4,128)(2,1)S(1)}, u32[]{:S(2)}, u32[]{:S(2)}) %collective-permute-start) | collective-permute-done | bytes 393248 | tf_op jit(solution)/shard_map/ppermute | solution.py:16
  34.1 2.6 fusion.2
  36.7 2.6 fusion.8
  39.4 2.9 %fusion.19 = f32[32,64,128]{2,1,0:T(8,128)S(1)} fusion(f32[32,64,128]{2,1,0:T(8,128)S(1)} %convolution_bitcast_fusion, f32[32,64,128]{2,1,0:T(8,128)S(1)} %fusion.2, f32[32,64,128]{2,1,0:T(8,128)S(1)} %fusion.8, bf16[2048,128,1]{0,1,2:T(8,128)(2,1)S(1)} %bitcast.57, bf16[32,64,2048]{2,1,0:T(8,128)(2,1)S(1)} %bitcast.47, ...), kind=kOutput, calls=%fused_computation.31 | convolution fusion | flops 1091305472 | bytes 13500416 | tf_op jit(solution)/shard_map/isn,nq->isq/dot_general | solution.py:28
  42.3 0.6 copy.9
  42.9 0.2 fusion.25
  43.1 0.5 copy.10
  43.7 0.2 reshape.179
  43.9 7.5 %all_to_all.18 = bf16[32,32,128]{2,1,0:T(8,128)(2,1)S(1)} all-to-all(bf16[32,32,128]{2,1,0:T(8,128)(2,1)S(1)} %reshape.179), channel_id=1, replica_groups=mesh['chan'=4,'pair'=16,'tm'=4] {'chan'}, dimensions={0} | all-to-all | bytes 524288 | tf_op jit(solution)/shard_map/all_to_all | solution.py:76
  51.4 0.7 copy.11
  52.1 0.0 all-gather.2.cloned.1.call-update
  52.2 0.0 reduce-scatter.2.cloned.1.call-start
  52.2 104.1 %all-gather.2.cloned.1.call-done = bf16[8,2048,128]{2,1,0:T(8,128)(2,1)} async-done(((bf16[8,128,128]{2,1,0:T(8,128)(2,1)}), bf16[8,2048,128]{2,1,0:T(8,128)(2,1)}) %all-gather.2.cloned.1.call-update) | async-done | bytes 4194320 | tf_op jit(solution)/shard_map/all_gather | solution.py:78
  156.3 6.4 %copy.12 = bf16[8,2048,128]{1,2,0:T(8,128)(2,1)} copy(bf16[8,2048,128]{2,1,0:T(8,128)(2,1)} %all-gather.2.cloned.1.call-done) | data formatting | bytes 8388608 | tf_op jit(solution)/shard_map/all_gather | solution.py:78
  162.7 2.5 slice_negate_fusion
  165.2 2.4 pad_maximum_fusion.3
  167.6 0.0 copy-start.1
  167.6 6.5 %copy.13 = bf16[1,8,2048,128]{3,2,1,0:T(8,128)(2,1)} copy(bf16[1,8,2048,128]{2,3,1,0:T(8,128)(2,1)} %bitcast.49) | data formatting | bytes 8388608 | tf_op jit(solution)/shard_map/stack;reshape | solution.py:53
  174.1 0.0 copy-done.1
  174.1 6.7 %convert_bitcast_fusion = bf16[2,8,128,2048]{2,3,0,1:T(8,128)(2,1)} fusion(bf16[8,128,128,1]{2,1,3,0:T(8,128)(2,1)S(1)} %bitcast.55, bf16[1,8,2048,128]{3,2,1,0:T(8,128)(2,1)} %copy.13, bf16[1,8,2048,128]{3,2,1,0:T(8,128)(2,1)} %bitcast.52), kind=kOutput, calls=%fused_computation.12 | convolution fusion | flops 1082130432 | bytes 17039360 | tf_op jit(solution)/shard_map/cis,rcjs->rcij/dot_general | solution.py:54
  180.8 0.0 reduce-scatter.2.cloned.1.call-update
  180.8 80.6 %reduce-scatter.2.cloned.1.call-done = bf16[2,8,128,512]{2,3,0,1:T(8,128)(2,1)} async-done(((bf16[2,8,128,2048]{2,3,0,1:T(8,128)(2,1)}), bf16[2,8,128,512]{2,3,0,1:T(8,128)(2,1)}) %reduce-scatter.2.cloned.1.call-update) | async-done | bytes 2097168 | tf_op jit(solution)/shard_map/reduce_scatter | solution.py:80
  261.5 4.0 %convert_multiply_fusion = f32[2,8,128,512]{2,3,0,1:T(8,128)} fusion(bf16[2,8,128,512]{2,3,0,1:T(8,128)(2,1)} %reduce-scatter.2.cloned.1.call-done), kind=kLoop, calls=%fused_computation.16 | loop fusion | flops 2097152 | bytes 6291456 | tf_op jit(solution)/shard_map/mul | solution.py:80
  265.5 5.3 %copy.15 = f32[2,8,128,512]{3,2,1,0:T(8,128)} copy(f32[2,8,128,512]{2,3,0,1:T(8,128)} %convert_multiply_fusion) | data formatting | bytes 8388608 | tf_op jit(solution)/shard_map/mul | solution.py:80
  (1 shorter events, 0.0 us)
Async XLA Ops:
  6.5 149.8 %all-gather.2.cloned.1.call-start = ((), (), s32[]{:S(2)}) async-start(), calls=%async_computation.2 | async-start | bytes 4456448 | tf_op jit(solution)/shard_map/all_gather | solution.py:78
  6.5 17.0 %copy-start.2 = (s32[32]{0:T(128)S(1)}, s32[32]{0:T(128)}, u32[]{:S(2)}) copy-start(s32[32]{0:T(128)} %param.3) | copy-start | bytes 388
  19.5 14.7 %collective-permute-start = (bf16[32,3,2048]{2,1,0:T(4,128)(2,1)S(1)}, bf16[32,3,2048]{2,1,0:T(4,128)(2,1)S(1)}, u32[]{:S(2)}, u32[]{:S(2)}) collective-permute-start(bf16[32,3,2048]{2,1,0:T(4,128)(2,1)S(1)} %slice.52), channel_id=1, source_target_pairs={{0,1},{1,2},{2,3},{4,5},{5,6},{6,7},{8,9},{9,10},{10,11},{12,13},{... | collective-permute-start | bytes 1179656 | tf_op jit(solution)/shard_map/ppermute | solution.py:16
  24.8 3.4 %copy-start = (bf16[4,8,64,2048]{3,2,1,0:T(8,128)(2,1)S(1)}, bf16[4,8,64,2048]{3,2,1,0:T(8,128)(2,1)}, u32[]{:S(2)}) copy-start(bf16[4,8,64,2048]{3,2,1,0:T(8,128)(2,1)} %copy.25) | copy-start | bytes 25165828
  52.2 209.3 %reduce-scatter.2.cloned.1.call-start = ((), (), s32[]{:S(2)}) async-start(), calls=%async_computation.3 | async-start | bytes 10485760 | tf_op jit(solution)/shard_map/reduce_scatter | solution.py:80
  167.6 6.5 %copy-start.1 = (bf16[8,4,32,128]{3,2,1,0:T(8,128)(2,1)S(1)}, bf16[8,4,32,128]{3,2,1,0:T(8,128)(2,1)}, u32[]{:S(2)}) copy-start(bf16[8,4,32,128]{3,2,1,0:T(8,128)(2,1)} %copy.11) | copy-start | bytes 786436
Sparse Core Ops, SparseCore 0:
  52.3 103.9 all-gather.1
  181.0 80.4 reduce-scatter.1
where the time goes:
time: 279 us; the launch traced here: 278 us
  waiting for transfers between devices  188 us (67%)
  local copies, waits for them, and re-layouts  36.1 us (13%)
  matrix products  17.3 us (6%)
  between operations  13.5 us (5%)
  other arithmetic  11.4 us (4%)
  blocking collectives  7.47 us (3%)
  starting transfers between devices  3.74 us (1%)
    all_gather x1, waiting for transfers between devices, body(): lax.all_gather(turned, 'pair', axis=1, tiled=True)  104 us
    reduce_scatter x1, waiting for transfers between devices, body(): lax.psum_scatter(partial_sums.astype(jnp.bfloat16), 'tm', scatter_dimensi...  80.6 us
    unnamed x7, local copies, waits for them, and re-layouts  14.1 us
    dot_general x3, matrix products, transform(): jnp.einsum('isn,nq->isq', extended[:, tap_index:tap_index + frame_count,...  7.62 us
    all_to_all x1, blocking collectives, body(): lax.all_to_all(rounded, 'chan', split_axis=0, concat_axis=1, tiled=True)  7.47 us
    dot_general x1, matrix products, correlate(): jnp.einsum('cis,rcjs->rcij', own_rows, paired, preferred_element_type=jnp...  6.73 us
    another operation x1, local copies, waits for them, and re-layouts, correlate(): paired = jnp.stack([columns, swap_parts(columns, segments)], axis=0)  6.5 us
    all_gather x1, local copies, waits for them, and re-layouts, body(): lax.all_gather(turned, 'pair', axis=1, tiled=True)  6.43 us
  transfers between devices with their start and end apart: 3, of which 3 were waited for; matrix products, arithmetic and copies ran while one was open for 2% of the time, Pallas kernels for 0%

commit v1 on v0

v1 whole, which is shorter than its diff:
```python
import math

import jax
import jax.numpy as jnp
import numpy as np
from jax import lax
from jax.experimental import pallas as pl
from jax.experimental.pallas import tpu as pltpu
from jax.sharding import Mesh
from jax.sharding import PartitionSpec as P

NFFT = 2048
TAPS = 4
NSEL = 32
LANES = 128
MIB = 1 << 20


def shifted(count, distance):
    return [(i, (i + distance) % count) for i in range(count)]


def filter_taps():
    position = (
        lax.broadcasted_iota(jnp.int32, (8, NFFT), 0) * NFFT
        + lax.broadcasted_iota(jnp.int32, (8, NFFT), 1)
    ).astype(jnp.float32) + 0.5
    turn = math.pi * (position / NFFT - TAPS / 2.0)
    hann_part = 0.5 - 0.5 * jnp.cos(2.0 * math.pi * position / (TAPS * NFFT))
    return jnp.sin(turn) / turn * hann_part


def signed_angle(phase):
    folded = ((phase + NFFT // 2) & (NFFT - 1)) - NFFT // 2
    return folded.astype(jnp.float32) * (2.0 * math.pi / NFFT)


def table_kernel(order, sel_hbm, volt_ref, table_ref, spill_ref, sel_ref, tail_ref, sems):
    reach = tail_ref.shape[2]
    fetch = pltpu.make_async_copy(sel_hbm, sel_ref, sems.at[0])
    fetch.start()
    last = pltpu.make_async_copy(
        volt_ref.at[:, :, pl.ds(volt_ref.shape[2] - reach, reach)], tail_ref, sems.at[1]
    )
    last.start()
    window = filter_taps().T
    fetch.wait()
    lane = lax.broadcasted_iota(jnp.int32, (1, LANES), 1)
    slot = lane & (NSEL - 1)
    sel = jnp.zeros((1, LANES), jnp.int32)
    for position, channel in enumerate(order):
        sel = jnp.where(slot == position, sel_ref[channel], sel)
    quarter = jnp.where((lane & NSEL) != 0, NFFT // 4, 0)
    coarse = lax.broadcasted_iota(jnp.int32, (32, LANES), 0) * 64
    fine = lax.broadcasted_iota(jnp.int32, (64, LANES), 0)
    coarse_angle = signed_angle(coarse * sel)
    fine_angle = signed_angle(fine * sel + quarter)
    coarse_cos, coarse_sin = jnp.cos(coarse_angle), jnp.sin(coarse_angle)
    fine_cos, fine_sin = jnp.cos(fine_angle), jnp.sin(fine_angle)
    upper_lane = lax.broadcasted_iota(jnp.int32, (64, LANES), 1) < LANES // 2
    for a in range(32):
        wave = coarse_cos[a : a + 1, :] * fine_cos - coarse_sin[a : a + 1, :] * fine_sin
        rows = slice(64 * a, 64 * (a + 1))
        for tap in range(TAPS):
            exact = window[rows, tap : tap + 1] * wave
            upper = exact.astype(jnp.bfloat16).astype(jnp.float32)
            table_ref[rows, LANES * tap : LANES * (tap + 1)] = jnp.where(
                upper_lane, upper, exact - upper
            ).astype(jnp.bfloat16)
    last.wait()
    inputs = tail_ref.shape[1]
    product = jnp.dot(
        jnp.concatenate(
            [tail_ref[0, :, NFFT * f : NFFT * (f + 1)] for f in range(TAPS - 1)], axis=0
        ),
        table_ref[...],
        preferred_element_type=jnp.float32,
    )
    for spectrum in range(TAPS - 1):
        total = jnp.zeros((inputs, LANES), jnp.float32)
        for f in range(spectrum, TAPS - 1):
            tap = f - spectrum
            total += product[inputs * f : inputs * (f + 1), LANES * tap : LANES * (tap + 1)]
        spill_ref[inputs * spectrum : inputs * (spectrum + 1), :] = total


def filter_kernel(batch, volt_ref, table_ref, out_ref, held, sems):
    inputs = held.shape[1]
    frames = held.shape[2] // NFFT
    reach = (TAPS - 1) * inputs
    rows = batch * inputs
    copies = []
    for first in range(0, frames, batch):
        part = pl.ds(first * NFFT, batch * NFFT)
        copy = pltpu.make_async_copy(
            volt_ref.at[:, :, part], held.at[:, :, part], sems.at[first // batch]
        )
        copy.start()
        copies.append(copy)
    out_ref[...] = jnp.zeros_like(out_ref)
    for first in range(0, frames, batch):
        copies[first // batch].wait()
        stacked = jnp.concatenate(
            [held[0, :, NFFT * f : NFFT * (f + 1)] for f in range(first, first + batch)], axis=0
        )
        product = jnp.dot(stacked, table_ref[...], preferred_element_type=jnp.float32)
        for tap in range(TAPS):
            start = first * inputs + reach - tap * inputs
            out_ref[start : start + rows, :] += product[:, LANES * tap : LANES * (tap + 1)]


def turn_kernel(spectra, total_ref, halo_ref, out_ref, joined, turned):
    inputs = out_ref.shape[1]
    factor = 1.0 / (24.0 * math.sqrt(NFFT))
    halo_rows = halo_ref.shape[0]
    head = total_ref[0:halo_rows, :] + halo_ref[...]
    body = total_ref[halo_rows : spectra * inputs, :]
    joined[0:halo_rows, :] = (head + pltpu.roll(head, LANES // 2, 1)) * factor
    joined[halo_rows : spectra * inputs, :] = (body + pltpu.roll(body, LANES // 2, 1)) * factor
    low_lane = lax.broadcasted_iota(jnp.int32, (NSEL, LANES), 1) < LANES // 2
    for i in range(0, inputs, 2):
        pair = jnp.concatenate(
            [
                joined[pl.ds(i, spectra, stride=inputs), :],
                joined[pl.ds(i + 1, spectra, stride=inputs), :],
            ],
            axis=0,
        )
        flipped = pair.T
        real, imag = flipped[0:NSEL, :], flipped[NSEL : 2 * NSEL, :]
        turned[pl.ds(i, NSEL, stride=inputs), :] = jnp.where(
            low_lane, real, pltpu.roll(imag, LANES // 2, 1)
        )
        turned[pl.ds(i + 1, NSEL, stride=inputs), :] = jnp.where(
            low_lane, pltpu.roll(real, LANES // 2, 1), imag
        )

    out_ref[...] = turned[...].reshape(NSEL, inputs, LANES).astype(jnp.bfloat16)


def matrix(refs):
    groups, segments = refs[0].shape[:2]
    return jnp.concatenate(
        [
            jnp.concatenate([ref[g, t] for ref in refs for g in range(groups)], axis=0)
            for t in range(segments)
        ],
        axis=1,
    )


def correlate_kernel(scale, count, reach, place_ref, *refs):
    units, out_refs, products = refs[: 2 * count], refs[2 * count : -1], refs[-1]
    sides = 2
    planes = products.shape[0] // sides
    own = matrix(units[0:2])
    low_lane = lax.broadcasted_iota(jnp.int32, (own.shape[0], LANES), 1) < LANES // 2
    swapped = []
    for start in range(0, own.shape[1], LANES):
        rolled = pltpu.roll(own[:, start : start + LANES].astype(jnp.float32), LANES // 2, 1)
        swapped.append(jnp.where(low_lane, rolled, -rolled).astype(jnp.bfloat16))
    left = jnp.concatenate([own, jnp.concatenate(swapped, axis=1)], axis=0)
    span = own.shape[0]
    rows = span // sides
    for u in range(count):
        tile = lax.dot_general(
            left,
            matrix(units[2 * u : 2 * u + 2]),
            (((1,), (1,)), ((), ())),
            preferred_element_type=jnp.float32,
        )
        tile = (tile * scale).astype(jnp.bfloat16)
        origin = place_ref[2 + u]
        column = pl.multiple_of(origin % 2 * span, span)
        for side in range(sides):
            for part in range(2):
                start = span * part + rows * side
                products[planes * side + origin // 2, part, :, pl.ds(column, span)] = tile[
                    start : start + rows, :
                ]
    for (dx, dy), out_ref in zip(reach, out_refs, strict=True):
        side, plane = (place_ref[0] + dx) % sides, (place_ref[1] + dy) % planes
        out_ref[...] = products[planes * side + plane]


def widen_kernel(count, place_ref, *refs):
    pieces, out_ref, wide, sems = refs[:count], refs[count], refs[count + 1], refs[count + 2]
    copies = []
    for k in range(count):
        channel = place_ref[k]
        for part in range(2):
            wide[k, part] = pieces[k][part].astype(jnp.float32)
            copy = pltpu.make_async_copy(
                wide.at[k, part], out_ref.at[part, channel], sems.at[k, part]
            )
            copy.start()
            copies.append(copy)
    for copy in copies:
        copy.wait()


def vmem(count=1):
    return [pl.BlockSpec(memory_space=pltpu.VMEM)] * count


def smem():
    return pl.BlockSpec(memory_space=pltpu.SMEM)


def body(voltages, selected):
    inputs = voltages.shape[1]
    spectra = voltages.shape[2] // NFFT
    segments = lax.axis_size("y")
    sides = lax.axis_size("xhi")
    ring = lax.axis_size("z")
    here_z, here_x, here_y = (lax.axis_index(a) for a in ("z", "xhi", "y"))

    order = np.arange(NSEL).reshape(2, 2, 2, 4).transpose(2, 0, 1, 3).reshape(-1)
    tables, spill = pl.pallas_call(
        lambda *refs: table_kernel([int(c) for c in order], *refs),
        in_specs=[pl.BlockSpec(memory_space=pl.ANY)] * 2,
        out_specs=vmem(2),
        out_shape=[
            jax.ShapeDtypeStruct((NFFT, TAPS * LANES), jnp.bfloat16),
            jax.ShapeDtypeStruct(((TAPS - 1) * inputs, LANES), jnp.float32),
        ],
        scratch_shapes=[
            pltpu.SMEM((NSEL,), jnp.int32),
            pltpu.VMEM((1, inputs, (TAPS - 1) * NFFT), jnp.bfloat16),
            pltpu.SemaphoreType.DMA((2,)),
        ],
        compiler_params=pltpu.CompilerParams(vmem_limit_bytes=46 * MIB),
        name="tables",
    )(selected, voltages)
    halo = lax.ppermute(spill, "y", [(i, i + 1) for i in range(segments - 1)])

    batch = 16
    filtered = pl.pallas_call(
        lambda *refs: filter_kernel(batch, *refs),
        in_specs=[pl.BlockSpec(memory_space=pl.ANY)] + vmem(),
        out_specs=vmem()[0],
        out_shape=jax.ShapeDtypeStruct(((spectra + TAPS - 1) * inputs, LANES), jnp.float32),
        scratch_shapes=[
            pltpu.VMEM(voltages.shape, voltages.dtype),
            pltpu.SemaphoreType.DMA((spectra // batch,)),
        ],
        compiler_params=pltpu.CompilerParams(vmem_limit_bytes=46 * MIB),
        cost_estimate=pl.CostEstimate(
            flops=2 * spectra * inputs * NFFT * TAPS * LANES,
            bytes_accessed=12 * MIB,
            transcendentals=0,
        ),
        name="filter_bank",
    )(voltages, tables)

    spectrum = pl.pallas_call(
        lambda *refs: turn_kernel(spectra, *refs),
        in_specs=vmem(2),
        out_specs=vmem()[0],
        out_shape=jax.ShapeDtypeStruct((NSEL, inputs, LANES), jnp.bfloat16),
        scratch_shapes=[
            pltpu.VMEM((spectra * inputs, LANES), jnp.float32),
            pltpu.VMEM((NSEL * inputs, LANES), jnp.float32),
        ],
        compiler_params=pltpu.CompilerParams(vmem_limit_bytes=8 * MIB),
        name="turn",
    )(filtered, halo)

    arrived = lax.all_to_all(
        spectrum, ("xhi", "xlo", "core", "y"), split_axis=0, concat_axis=0, tiled=True
    )
    own = arrived.reshape(8, segments, inputs, LANES)

    half = own.shape[0] // 2
    low, high = own[:half], own[half:]
    units = [low, high]
    right_low = left_low = low
    right_high = left_high = high
    for _ in range(ring // 2 - 1):
        right_low = lax.ppermute(right_low, "z", shifted(ring, 1))
        left_high = lax.ppermute(left_high, "z", shifted(ring, -1))
        right_high = lax.ppermute(right_high, "z", shifted(ring, 1))
        left_low = lax.ppermute(left_low, "z", shifted(ring, -1))
        units += [right_low, right_high, left_low, left_high]
    units.append(lax.ppermute(right_low, "z", shifted(ring, 1)))
    units.append(lax.ppermute(left_high, "z", shifted(ring, -1)))
    offsets = [0]
    for d in range(1, ring // 2):
        offsets += [-d, d]
    offsets.append(ring // 2)
    origin = [(here_z + d) % ring for d in offsets]

    scale = 1.0 / (spectra * segments)
    rows = half * inputs
    reach = ((1, 2), (0, 2), (1, 1), (1, 3), (0, 1), (0, 3), (1, 0), (0, 0))
    place = jnp.stack([here_x, here_y] + origin).astype(jnp.int32)
    products = pl.pallas_call(
        lambda *refs: correlate_kernel(scale, len(origin), reach, *refs),
        in_specs=[smem()] + vmem(len(units)),
        out_specs=vmem(len(reach)),
        out_shape=[jax.ShapeDtypeStruct((2, rows, 4 * rows), jnp.bfloat16)] * len(reach),
        scratch_shapes=[pltpu.VMEM((len(reach), 2, rows, 4 * rows), jnp.bfloat16)],
        compiler_params=pltpu.CompilerParams(vmem_limit_bytes=12 * MIB),
        name="correlate",
    )(place, *units)
    pieces, channels = [], []
    for (dx, dy), product in zip(reach, products, strict=True):
        if dx or dy:
            route = [
                (x * segments + y, (x + dx) % sides * segments + (y + dy) % segments)
                for x in range(sides)
                for y in range(segments)
            ]
            product = lax.ppermute(product, ("xhi", "y"), route)
        pieces.append(product)
        channels.append((here_x - dx) % sides * segments + (here_y - dy) % segments)

    return pl.pallas_call(
        lambda *refs: widen_kernel(len(pieces), *refs),
        in_specs=[smem()] + vmem(len(pieces)),
        out_specs=pl.BlockSpec(memory_space=pl.ANY),
        out_shape=jax.ShapeDtypeStruct((2, len(pieces), rows, 4 * rows), jnp.float32),
        scratch_shapes=[
            pltpu.VMEM((len(pieces), 2, rows, 4 * rows), jnp.float32),
            pltpu.SemaphoreType.DMA((len(pieces), 2)),
        ],
        compiler_params=pltpu.CompilerParams(vmem_limit_bytes=10 * MIB),
        name="widen",
    )(jnp.stack(channels).astype(jnp.int32), *pieces)


def solution(mesh):
    fine = Mesh(mesh.devices.reshape(2, 2, 8, 2, 4), ("xlo", "core", "z", "xhi", "y"))
    return jax.shard_map(
        body,
        mesh=fine,
        in_specs=(P(("z", "xhi"), ("xlo", "core"), "y"), P()),
        out_specs=P(None, ("xlo", "core"), ("z", "xhi"), "y"),
        check_vma=False,
    )
```

time: 279 us -> 96.2 us (0.34)
  waiting for transfers between devices: 188 us -> 24.1 us
  starting transfers between devices: 3.74 us -> 39.1 us
  local copies, waits for them, and re-layouts: 36.1 us -> 0.84 us
  matrix products: 17.3 us -> 0 us
  Pallas kernels: 0 us -> 16 us
  between operations: 13.5 us -> 0.24 us
  other arithmetic: 11.4 us -> 0 us
  blocking collectives: 7.47 us -> 15 us
    all_gather x1 -> x0, waiting for transfers between devices: 104 us -> none  [body(): lax.all_gather(turned, 'pair', axis=1, tiled=True)]
    reduce_scatter x1 -> x0, waiting for transfers between devices: 80.6 us -> none  [body(): lax.psum_scatter(partial_sums.astype(jnp.bfloat16), 'tm', scatter_dimensi...]
    ppermute x1 -> x22, starting transfers between devices: 3.69 us -> 39.1 us  [the longest x7 12.4 us: body(): product = lax.ppermute(product, ('xhi', 'y'), route)]
    ppermute x1 -> x22, waiting for transfers between devices: 3.51 us -> 24.1 us  [the longest x7 16.7 us: body(): product = lax.ppermute(product, ('xhi', 'y'), route)]
    dot_general x5 -> x0, matrix products: 17.3 us -> none  [the longest x3 7.62 us: transform(): jnp.einsum('isn,nq->isq', extended[:, tap_index:tap_index + frame_count,...]
    pallas_call x0 -> x5, Pallas kernels: none -> 16 us  [the longest x1 6.69 us: body(): pl.pallas_call(lambda *refs: filter_kernel(batch, *refs), in_specs=[pl.Bl...]
    unnamed x7 -> x2, local copies, waits for them, and re-layouts: 14.1 us -> 0.65 us
    all_to_all x1, blocking collectives: 7.47 us -> 15 us  [body(): lax.all_to_all(spectrum, ('xhi', 'xlo', 'core', 'y'), split_axis=0, conca...]
  transfers between devices with their start and end apart: 3 -> 22, of which waited for: 3 -> 12; matrix products, arithmetic and copies ran while one was open for 2% -> 0% of each run, Pallas kernels for 0% -> 7%
where the time goes in v1:
time: 96.2 us; the launch traced here: 95.2 us
  starting transfers between devices  39.1 us (41%)
  waiting for transfers between devices  24.1 us (25%)
  Pallas kernels  16 us (17%)
  blocking collectives  15 us (16%)
    ppermute x7, waiting for transfers between devices, body(): product = lax.ppermute(product, ('xhi', 'y'), route)  16.7 us
    all_to_all x1, blocking collectives, body(): lax.all_to_all(spectrum, ('xhi', 'xlo', 'core', 'y'), split_axis=0, conca...  15 us
    ppermute x7, starting transfers between devices, body(): product = lax.ppermute(product, ('xhi', 'y'), route)  12.4 us
    ppermute x3, starting transfers between devices, body(): left_high = lax.ppermute(left_high, 'z', shifted(ring, -1))  11.4 us
    pallas_call x1, Pallas kernels, body(): pl.pallas_call(lambda *refs: filter_kernel(batch, *refs), in_specs=[pl.Bl...  6.69 us
    ppermute x3, starting transfers between devices, body(): left_low = lax.ppermute(left_low, 'z', shifted(ring, -1))  5.58 us
    ppermute x3, waiting for transfers between devices, body(): right_low = lax.ppermute(right_low, 'z', shifted(ring, 1))  4.02 us
    ppermute x1, starting transfers between devices, body(): units.append(lax.ppermute(left_high, 'z', shifted(ring, -1)))  3.69 us
  transfers between devices with their start and end apart: 22, of which 12 were waited for; matrix products, arithmetic and copies ran while one was open for 0% of the time, Pallas kernels for 7%

profile of v1, /device:TPU:2, one launch (start us, length us, event | category | flops | bytes accessed | tf_op | source)
XLA Modules:
  0.0 95.2 jit_solution(14784567500517216663)
XLA Ops:
  0.0 0.0 copy-start
  0.0 0.7 copy-done
  0.7 2.5 %tables.1 = (bf16[2048,512]{1,0:T(8,128)(2,1)S(1)}, f32[96,128]{1,0:T(8,128)S(1)}) custom-call(s32[32]{0:T(128)S(1)} %copy-done, bf16[1,32,131072]{2,1,0:T(8,128)(2,1)} %refs_0_.3), custom_call_target="tpu_custom_call" | custom-call | tf_op jit(solution)/shard_map/tables/pallas_call | solution.py:219
  3.1 3.5 %collective-permute-start = (f32[96,128]{1,0:T(8,128)S(1)}, f32[96,128]{1,0:T(8,128)S(1)}, u32[]{:S(2)}, u32[]{:S(2)}) collective-permute-start(f32[96,128]{1,0:T(8,128)S(1)} %get-tuple-element.16), channel_id=1, source_target_pairs={{0,1},{1,2},{2,3},{4,5},{5,6},{6,7},{8,9},{9,10},{10,11},{12,13},{... | collective-permute-start | bytes 147464 | tf_op jit(solution)/shard_map/ppermute | solution.py:235
  6.6 6.7 %filter_bank.1.refs_0_ = f32[2144,128]{1,0:T(8,128)S(1)} custom-call(bf16[1,32,131072]{2,1,0:T(8,128)(2,1)} %refs_0_.3, bf16[2048,512]{1,0:T(8,128)(2,1)S(1)} %get-tuple-element.15.refs_1_), custom_call_target="tpu_custom_call" | custom-call | flops 4294967296 | bytes 12582912 | tf_op jit(solution)/shard_map/filter_bank/pallas_call | solution.py:238
  13.3 0.0 collective-permute-done.refs_1_
  13.3 1.4 %turn.1 = bf16[32,32,128]{2,1,0:T(8,128)(2,1)S(1)} custom-call(f32[2144,128]{1,0:T(8,128)S(1)} %filter_bank.1.refs_0_, f32[96,128]{1,0:T(8,128)S(1)} %collective-permute-done.refs_1_), custom_call_target="tpu_custom_call" | custom-call | tf_op jit(solution)/shard_map/turn/pallas_call | solution.py:256
  14.7 15.0 %all_to_all.5 = bf16[32,32,128]{2,1,0:T(8,128)(2,1)S(1)} all-to-all(bf16[32,32,128]{2,1,0:T(8,128)(2,1)S(1)} %turn.1), channel_id=1, replica_groups=mesh['xlo'=2,'core'=2,'z'=8,'xhi'=2,'y'=4] {'xhi','xlo','core','y'}, dimensions={0} | all-to-all | bytes 524288 | tf_op jit(solution)/shard_map/all_to_all | solution.py:269
  29.8 2.0 %collective-permute-start.1 = (bf16[4,4,32,128]{3,2,1,0:T(8,128)(2,1)S(1)}, bf16[4,4,32,128]{3,2,1,0:T(8,128)(2,1)S(1)}, u32[]{:S(2)}, u32[]{:S(2)}) collective-permute-start(bf16[4,4,32,128]{3,2,1,0:T(8,128)(2,1)S(1)} %bitcast.23), channel_id=1, source_target_pairs={{0,8},{8,16},{16,24},{24,32},{32,40},{40,48},{48,56},{56,0},{1,9},... | collective-permute-start | bytes 393224 | tf_op jit(solution)/shard_map/ppermute | solution.py:280
  31.8 4.0 %collective-permute-start.4 = (bf16[4,4,32,128]{3,2,1,0:T(8,128)(2,1)S(1)}, bf16[4,4,32,128]{3,2,1,0:T(8,128)(2,1)S(1)}, u32[]{:S(2)}, u32[]{:S(2)}) collective-permute-start(bf16[4,4,32,128]{3,2,1,0:T(8,128)(2,1)S(1)} %bitcast.20), channel_id=1, source_target_pairs={{0,56},{8,0},{16,8},{24,16},{32,24},{40,32},{48,40},{56,48},{1,57}... | collective-permute-start | bytes 393224 | tf_op jit(solution)/shard_map/ppermute | solution.py:281
  35.8 1.9 %collective-permute-start.3 = (bf16[4,4,32,128]{3,2,1,0:T(8,128)(2,1)S(1)}, bf16[4,4,32,128]{3,2,1,0:T(8,128)(2,1)S(1)}, u32[]{:S(2)}, u32[]{:S(2)}) collective-permute-start(bf16[4,4,32,128]{3,2,1,0:T(8,128)(2,1)S(1)} %bitcast.24), channel_id=1, source_target_pairs={{0,56},{8,0},{16,8},{24,16},{32,24},{40,32},{48,40},{56,48},{1,57}... | collective-permute-start | bytes 393224 | tf_op jit(solution)/shard_map/ppermute | solution.py:283
  37.7 0.1 collective-permute-start.2
  37.8 1.7 %collective-permute-done.1.refs_3_ = bf16[4,4,32,128]{3,2,1,0:T(8,128)(2,1)S(1)} collective-permute-done((bf16[4,4,32,128]{3,2,1,0:T(8,128)(2,1)S(1)}, bf16[4,4,32,128]{3,2,1,0:T(8,128)(2,1)S(1)}, u32[]{:S(2)}, u32[]{:S(2)}) %collective-permute-start.1) | collective-permute-done | bytes 131104 | tf_op jit(solution)/shard_map/ppermute | solution.py:280
  39.5 0.0 collective-permute-start.5
  39.5 0.2 collective-permute-done.4.refs_6_
  39.7 3.7 %collective-permute-start.8 = (bf16[4,4,32,128]{3,2,1,0:T(8,128)(2,1)S(1)}, bf16[4,4,32,128]{3,2,1,0:T(8,128)(2,1)S(1)}, u32[]{:S(2)}, u32[]{:S(2)}) collective-permute-start(bf16[4,4,32,128]{3,2,1,0:T(8,128)(2,1)S(1)} %collective-permute-done.4.refs_6_), channel_id=1, source_target_pairs={{0,56},{8,0},{16,8},{24,16},{32,24},{40,32},{48,40},{56,48},{1,57}... | collective-permute-start | bytes 393224 | tf_op jit(solution)/shard_map/ppermute | solution.py:281
  43.4 0.0 collective-permute-done.3.refs_5_
  43.4 2.0 %collective-permute-start.7 = (bf16[4,4,32,128]{3,2,1,0:T(8,128)(2,1)S(1)}, bf16[4,4,32,128]{3,2,1,0:T(8,128)(2,1)S(1)}, u32[]{:S(2)}, u32[]{:S(2)}) collective-permute-start(bf16[4,4,32,128]{3,2,1,0:T(8,128)(2,1)S(1)} %collective-permute-done.3.refs_5_), channel_id=1, source_target_pairs={{0,56},{8,0},{16,8},{24,16},{32,24},{40,32},{48,40},{56,48},{1,57}... | collective-permute-start | bytes 393224 | tf_op jit(solution)/shard_map/ppermute | solution.py:283
  45.3 0.0 collective-permute-done.2.refs_4_
  45.3 0.1 collective-permute-start.6
  45.4 1.3 %collective-permute-done.5.refs_7_ = bf16[4,4,32,128]{3,2,1,0:T(8,128)(2,1)S(1)} collective-permute-done((bf16[4,4,32,128]{3,2,1,0:T(8,128)(2,1)S(1)}, bf16[4,4,32,128]{3,2,1,0:T(8,128)(2,1)S(1)}, u32[]{:S(2)}, u32[]{:S(2)}) %collective-permute-start.5) | collective-permute-done | bytes 131104 | tf_op jit(solution)/shard_map/ppermute | solution.py:280
  46.7 0.0 collective-permute-start.9
  46.7 0.2 collective-permute-done.8.refs_10_
  47.0 3.7 %collective-permute-start.12 = (bf16[4,4,32,128]{3,2,1,0:T(8,128)(2,1)S(1)}, bf16[4,4,32,128]{3,2,1,0:T(8,128)(2,1)S(1)}, u32[]{:S(2)}, u32[]{:S(2)}) collective-permute-start(bf16[4,4,32,128]{3,2,1,0:T(8,128)(2,1)S(1)} %collective-permute-done.8.refs_10_), channel_id=1, source_target_pairs={{0,56},{8,0},{16,8},{24,16},{32,24},{40,32},{48,40},{56,48},{1,57}... | collective-permute-start | bytes 393224 | tf_op jit(solution)/shard_map/ppermute | solution.py:281
  50.7 0.0 collective-permute-done.7.refs_9_
  50.7 1.7 %collective-permute-start.11 = (bf16[4,4,32,128]{3,2,1,0:T(8,128)(2,1)S(1)}, bf16[4,4,32,128]{3,2,1,0:T(8,128)(2,1)S(1)}, u32[]{:S(2)}, u32[]{:S(2)}) collective-permute-start(bf16[4,4,32,128]{3,2,1,0:T(8,128)(2,1)S(1)} %collective-permute-done.7.refs_9_), channel_id=1, source_target_pairs={{0,56},{8,0},{16,8},{24,16},{32,24},{40,32},{48,40},{56,48},{1,57}... | collective-permute-start | bytes 393224 | tf_op jit(solution)/shard_map/ppermute | solution.py:283
  52.3 0.0 collective-permute-done.6.refs_8_
  52.3 0.4 collective-permute-start.10
  52.7 1.0 %collective-permute-done.9.refs_11_ = bf16[4,4,32,128]{3,2,1,0:T(8,128)(2,1)S(1)} collective-permute-done((bf16[4,4,32,128]{3,2,1,0:T(8,128)(2,1)S(1)}, bf16[4,4,32,128]{3,2,1,0:T(8,128)(2,1)S(1)}, u32[]{:S(2)}, u32[]{:S(2)}) %collective-permute-start.9) | collective-permute-done | bytes 131104 | tf_op jit(solution)/shard_map/ppermute | solution.py:280
  53.7 0.0 collective-permute-start.13
  53.7 0.5 collective-permute-done.12.refs_14_
  54.2 3.7 %collective-permute-start.14 = (bf16[4,4,32,128]{3,2,1,0:T(8,128)(2,1)S(1)}, bf16[4,4,32,128]{3,2,1,0:T(8,128)(2,1)S(1)}, u32[]{:S(2)}, u32[]{:S(2)}) collective-permute-start(bf16[4,4,32,128]{3,2,1,0:T(8,128)(2,1)S(1)} %collective-permute-done.12.refs_14_), channel_id=1, source_target_pairs={{0,56},{8,0},{16,8},{24,16},{32,24},{40,32},{48,40},{56,48},{1,57}... | collective-permute-start | bytes 393224 | tf_op jit(solution)/shard_map/ppermute | solution.py:286
  57.9 0.1 stack.79.refs_0_
  58.0 0.0 collective-permute-done.11.refs_13_
  58.0 1.0 %collective-permute-done.10.refs_12_ = bf16[4,4,32,128]{3,2,1,0:T(8,128)(2,1)S(1)} collective-permute-done((bf16[4,4,32,128]{3,2,1,0:T(8,128)(2,1)S(1)}, bf16[4,4,32,128]{3,2,1,0:T(8,128)(2,1)S(1)}, u32[]{:S(2)}, u32[]{:S(2)}) %collective-permute-start.10) | collective-permute-done | bytes 131104 | tf_op jit(solution)/shard_map/ppermute | solution.py:282
  59.1 1.4 %collective-permute-done.13.refs_15_ = bf16[4,4,32,128]{3,2,1,0:T(8,128)(2,1)S(1)} collective-permute-done((bf16[4,4,32,128]{3,2,1,0:T(8,128)(2,1)S(1)}, bf16[4,4,32,128]{3,2,1,0:T(8,128)(2,1)S(1)}, u32[]{:S(2)}, u32[]{:S(2)}) %collective-permute-start.13) | collective-permute-done | bytes 131104 | tf_op jit(solution)/shard_map/ppermute | solution.py:285
  60.5 0.0 collective-permute-done.14.refs_16_
  60.5 2.7 %correlate.1 = (bf16[2,128,512]{2,1,0:T(8,128)(2,1)S(1)}, bf16[2,128,512]{2,1,0:T(8,128)(2,1)S(1)}, bf16[2,128,512]{2,1,0:T(8,128)(2,1)}, bf16[2,128,512]{2,1,0:...) custom-call(s32[10]{0:T(128)S(1)} %stack.79.refs_0_, ...), custom_call_target="tpu_custom_call" | custom-call | tf_op jit(solution)/shard_map/correlate/pallas_call | solution.py:297
  63.2 1.6 %collective-permute-start.15 = (bf16[2,128,512]{2,1,0:T(8,128)(2,1)S(1)}, bf16[2,128,512]{2,1,0:T(8,128)(2,1)S(1)}, u32[]{:S(2)}, u32[]{:S(2)}) collective-permute-start(bf16[2,128,512]{2,1,0:T(8,128)(2,1)S(1)} %get-tuple-element.17), channel_id=1, source_target_pairs={{0,6},{1,7},{2,4},{3,5},{4,2},{5,3},{6,0},{7,1},{8,14},{9,15},{10,... | collective-permute-start | bytes 786440 | tf_op jit(solution)/shard_map/ppermute | solution.py:314
  64.8 2.8 %collective-permute-start.16 = (bf16[2,128,512]{2,1,0:T(8,128)(2,1)S(1)}, bf16[2,128,512]{2,1,0:T(8,128)(2,1)S(1)}, u32[]{:S(2)}, u32[]{:S(2)}) collective-permute-start(bf16[2,128,512]{2,1,0:T(8,128)(2,1)S(1)} %get-tuple-element.18), channel_id=1, source_target_pairs={{0,2},{1,3},{2,0},{3,1},{4,6},{5,7},{6,4},{7,5},{8,10},{9,11},{10,... | collective-permute-start | bytes 786440 | tf_op jit(solution)/shard_map/ppermute | solution.py:314
  67.6 2.5 %collective-permute-start.17 = (bf16[2,128,512]{2,1,0:T(8,128)(2,1)}, bf16[2,128,512]{2,1,0:T(8,128)(2,1)S(1)}, u32[]{:S(2)}, u32[]{:S(2)}) collective-permute-start(bf16[2,128,512]{2,1,0:T(8,128)(2,1)} %get-tuple-element.19), channel_id=1, source_target_pairs={{0,5},{1,6},{2,7},{3,4},{4,1},{5,2},{6,3},{7,0},{8,13},{9,14},{10,... | collective-permute-start | bytes 786440 | tf_op jit(solution)/shard_map/ppermute | solution.py:314
  70.1 3.2 %collective-permute-start.18 = (bf16[2,128,512]{2,1,0:T(8,128)(2,1)S(1)}, bf16[2,128,512]{2,1,0:T(8,128)(2,1)S(1)}, u32[]{:S(2)}, u32[]{:S(2)}) collective-permute-start(bf16[2,128,512]{2,1,0:T(8,128)(2,1)S(1)} %get-tuple-element.20), channel_id=1, source_target_pairs={{0,7},{1,4},{2,5},{3,6},{4,3},{5,0},{6,1},{7,2},{8,15},{9,12},{10,... | collective-permute-start | bytes 786440 | tf_op jit(solution)/shard_map/ppermute | solution.py:314
  73.2 0.0 collective-permute-start.19
  73.2 4.0 %collective-permute-done.15.refs_1_ = bf16[2,128,512]{2,1,0:T(8,128)(2,1)S(1)} collective-permute-done((bf16[2,128,512]{2,1,0:T(8,128)(2,1)S(1)}, bf16[2,128,512]{2,1,0:T(8,128)(2,1)S(1)}, u32[]{:S(2)}, u32[]{:S(2)}) %collective-permute-start.15) | collective-permute-done | bytes 262176 | tf_op jit(solution)/shard_map/ppermute | solution.py:314
  77.2 0.0 collective-permute-start.20
  77.2 7.3 %collective-permute-done.16.refs_2_ = bf16[2,128,512]{2,1,0:T(8,128)(2,1)S(1)} collective-permute-done((bf16[2,128,512]{2,1,0:T(8,128)(2,1)S(1)}, bf16[2,128,512]{2,1,0:T(8,128)(2,1)S(1)}, u32[]{:S(2)}, u32[]{:S(2)}) %collective-permute-start.16) | collective-permute-done | bytes 262176 | tf_op jit(solution)/shard_map/ppermute | solution.py:314
  84.5 2.4 %collective-permute-start.21 = (bf16[2,128,512]{2,1,0:T(8,128)(2,1)S(1)}, bf16[2,128,512]{2,1,0:T(8,128)(2,1)S(1)}, u32[]{:S(2)}, u32[]{:S(2)}) collective-permute-start(bf16[2,128,512]{2,1,0:T(8,128)(2,1)S(1)} %get-tuple-element.23), channel_id=1, source_target_pairs={{0,4},{1,5},{2,6},{3,7},{4,0},{5,1},{6,2},{7,3},{8,12},{9,13},{10,... | collective-permute-start | bytes 786440 | tf_op jit(solution)/shard_map/ppermute | solution.py:314
  86.9 0.1 stack.68.refs_0_
  87.0 0.0 collective-permute-done.17.refs_3_
  87.0 0.0 collective-permute-done.18.refs_4_
  87.0 2.2 %collective-permute-done.19.refs_5_ = bf16[2,128,512]{2,1,0:T(8,128)(2,1)S(1)} collective-permute-done((bf16[2,128,512]{2,1,0:T(8,128)(2,1)S(1)}, bf16[2,128,512]{2,1,0:T(8,128)(2,1)S(1)}, u32[]{:S(2)}, u32[]{:S(2)}) %collective-permute-start.19) | collective-permute-done | bytes 262176 | tf_op jit(solution)/shard_map/ppermute | solution.py:314
  89.2 0.0 collective-permute-done.20.refs_6_
  89.2 3.2 %collective-permute-done.21.refs_7_ = bf16[2,128,512]{2,1,0:T(8,128)(2,1)S(1)} collective-permute-done((bf16[2,128,512]{2,1,0:T(8,128)(2,1)S(1)}, bf16[2,128,512]{2,1,0:T(8,128)(2,1)S(1)}, u32[]{:S(2)}, u32[]{:S(2)}) %collective-permute-start.21) | collective-permute-done | bytes 262176 | tf_op jit(solution)/shard_map/ppermute | solution.py:314
  92.4 2.7 %widen.1 = f32[2,8,128,512]{3,2,1,0:T(8,128)} custom-call(s32[8]{0:T(128)S(1)} %stack.68.refs_0_, bf16[2,128,512]{2,1,0:T(8,128)(2,1)S(1)} %collective-permute-done.15.refs_1_, bf16[2,128,512]{2,1,0:T(8,128)(2,1)S(1)} %collective-permute-done.16.refs_2_, bf16[2,128,512]{2,1,0:T(8,128)(2,1)S(1)} %collective-permute-done.17.refs_3_, ...), custom_call_target="tpu_custom_call" | custom-call | tf_op jit(solution)/shard_map/widen/pallas_call | solution.py:318
  (1 shorter events, 0.0 us)
Async XLA Ops:
  0.0 0.7 copy-start
  3.1 10.2 %collective-permute-start = (f32[96,128]{1,0:T(8,128)S(1)}, f32[96,128]{1,0:T(8,128)S(1)}, u32[]{:S(2)}, u32[]{:S(2)}) collective-permute-start(f32[96,128]{1,0:T(8,128)S(1)} %get-tuple-element.16), channel_id=1, source_target_pairs={{0,1},{1,2},{2,3},{4,5},{5,6},{6,7},{8,9},{9,10},{10,11},{12,13},{... | collective-permute-start | bytes 147464 | tf_op jit(solution)/shard_map/ppermute | solution.py:235
  29.8 9.7 %collective-permute-start.1 = (bf16[4,4,32,128]{3,2,1,0:T(8,128)(2,1)S(1)}, bf16[4,4,32,128]{3,2,1,0:T(8,128)(2,1)S(1)}, u32[]{:S(2)}, u32[]{:S(2)}) collective-permute-start(bf16[4,4,32,128]{3,2,1,0:T(8,128)(2,1)S(1)} %bitcast.23), channel_id=1, source_target_pairs={{0,8},{8,16},{16,24},{24,32},{32,40},{40,48},{48,56},{56,0},{1,9},... | collective-permute-start | bytes 393224 | tf_op jit(solution)/shard_map/ppermute | solution.py:280
  31.8 7.9 %collective-permute-start.4 = (bf16[4,4,32,128]{3,2,1,0:T(8,128)(2,1)S(1)}, bf16[4,4,32,128]{3,2,1,0:T(8,128)(2,1)S(1)}, u32[]{:S(2)}, u32[]{:S(2)}) collective-permute-start(bf16[4,4,32,128]{3,2,1,0:T(8,128)(2,1)S(1)} %bitcast.20), channel_id=1, source_target_pairs={{0,56},{8,0},{16,8},{24,16},{32,24},{40,32},{48,40},{56,48},{1,57}... | collective-permute-start | bytes 393224 | tf_op jit(solution)/shard_map/ppermute | solution.py:281
  35.8 7.6 %collective-permute-start.3 = (bf16[4,4,32,128]{3,2,1,0:T(8,128)(2,1)S(1)}, bf16[4,4,32,128]{3,2,1,0:T(8,128)(2,1)S(1)}, u32[]{:S(2)}, u32[]{:S(2)}) collective-permute-start(bf16[4,4,32,128]{3,2,1,0:T(8,128)(2,1)S(1)} %bitcast.24), channel_id=1, source_target_pairs={{0,56},{8,0},{16,8},{24,16},{32,24},{40,32},{48,40},{56,48},{1,57}... | collective-permute-start | bytes 393224 | tf_op jit(solution)/shard_map/ppermute | solution.py:283
  37.7 7.6 %collective-permute-start.2 = (bf16[4,4,32,128]{3,2,1,0:T(8,128)(2,1)S(1)}, bf16[4,4,32,128]{3,2,1,0:T(8,128)(2,1)S(1)}, u32[]{:S(2)}, u32[]{:S(2)}) collective-permute-start(bf16[4,4,32,128]{3,2,1,0:T(8,128)(2,1)S(1)} %bitcast.21), channel_id=1, source_target_pairs={{0,8},{8,16},{16,24},{24,32},{32,40},{40,48},{48,56},{56,0},{1,9},... | collective-permute-start | bytes 393224 | tf_op jit(solution)/shard_map/ppermute | solution.py:282
  39.5 7.2 %collective-permute-start.5 = (bf16[4,4,32,128]{3,2,1,0:T(8,128)(2,1)S(1)}, bf16[4,4,32,128]{3,2,1,0:T(8,128)(2,1)S(1)}, u32[]{:S(2)}, u32[]{:S(2)}) collective-permute-start(bf16[4,4,32,128]{3,2,1,0:T(8,128)(2,1)S(1)} %collective-permute-done.1.refs_3_), channel_id=1, source_target_pairs={{0,8},{8,16},{16,24},{24,32},{32,40},{40,48},{48,56},{56,0},{1,9},... | collective-permute-start | bytes 393224 | tf_op jit(solution)/shard_map/ppermute | solution.py:280
  39.7 7.3 %collective-permute-start.8 = (bf16[4,4,32,128]{3,2,1,0:T(8,128)(2,1)S(1)}, bf16[4,4,32,128]{3,2,1,0:T(8,128)(2,1)S(1)}, u32[]{:S(2)}, u32[]{:S(2)}) collective-permute-start(bf16[4,4,32,128]{3,2,1,0:T(8,128)(2,1)S(1)} %collective-permute-done.4.refs_6_), channel_id=1, source_target_pairs={{0,56},{8,0},{16,8},{24,16},{32,24},{40,32},{48,40},{56,48},{1,57}... | collective-permute-start | bytes 393224 | tf_op jit(solution)/shard_map/ppermute | solution.py:281
  43.4 7.3 %collective-permute-start.7 = (bf16[4,4,32,128]{3,2,1,0:T(8,128)(2,1)S(1)}, bf16[4,4,32,128]{3,2,1,0:T(8,128)(2,1)S(1)}, u32[]{:S(2)}, u32[]{:S(2)}) collective-permute-start(bf16[4,4,32,128]{3,2,1,0:T(8,128)(2,1)S(1)} %collective-permute-done.3.refs_5_), channel_id=1, source_target_pairs={{0,56},{8,0},{16,8},{24,16},{32,24},{40,32},{48,40},{56,48},{1,57}... | collective-permute-start | bytes 393224 | tf_op jit(solution)/shard_map/ppermute | solution.py:283
  45.3 7.0 %collective-permute-start.6 = (bf16[4,4,32,128]{3,2,1,0:T(8,128)(2,1)S(1)}, bf16[4,4,32,128]{3,2,1,0:T(8,128)(2,1)S(1)}, u32[]{:S(2)}, u32[]{:S(2)}) collective-permute-start(bf16[4,4,32,128]{3,2,1,0:T(8,128)(2,1)S(1)} %collective-permute-done.2.refs_4_), channel_id=1, source_target_pairs={{0,8},{8,16},{16,24},{24,32},{32,40},{40,48},{48,56},{56,0},{1,9},... | collective-permute-start | bytes 393224 | tf_op jit(solution)/shard_map/ppermute | solution.py:282
  46.7 7.0 %collective-permute-start.9 = (bf16[4,4,32,128]{3,2,1,0:T(8,128)(2,1)S(1)}, bf16[4,4,32,128]{3,2,1,0:T(8,128)(2,1)S(1)}, u32[]{:S(2)}, u32[]{:S(2)}) collective-permute-start(bf16[4,4,32,128]{3,2,1,0:T(8,128)(2,1)S(1)} %collective-permute-done.5.refs_7_), channel_id=1, source_target_pairs={{0,8},{8,16},{16,24},{24,32},{32,40},{40,48},{48,56},{56,0},{1,9},... | collective-permute-start | bytes 393224 | tf_op jit(solution)/shard_map/ppermute | solution.py:280
  47.0 7.3 %collective-permute-start.12 = (bf16[4,4,32,128]{3,2,1,0:T(8,128)(2,1)S(1)}, bf16[4,4,32,128]{3,2,1,0:T(8,128)(2,1)S(1)}, u32[]{:S(2)}, u32[]{:S(2)}) collective-permute-start(bf16[4,4,32,128]{3,2,1,0:T(8,128)(2,1)S(1)} %collective-permute-done.8.refs_10_), channel_id=1, source_target_pairs={{0,56},{8,0},{16,8},{24,16},{32,24},{40,32},{48,40},{56,48},{1,57}... | collective-permute-start | bytes 393224 | tf_op jit(solution)/shard_map/ppermute | solution.py:281
  50.7 7.4 %collective-permute-start.11 = (bf16[4,4,32,128]{3,2,1,0:T(8,128)(2,1)S(1)}, bf16[4,4,32,128]{3,2,1,0:T(8,128)(2,1)S(1)}, u32[]{:S(2)}, u32[]{:S(2)}) collective-permute-start(bf16[4,4,32,128]{3,2,1,0:T(8,128)(2,1)S(1)} %collective-permute-done.7.refs_9_), channel_id=1, source_target_pairs={{0,56},{8,0},{16,8},{24,16},{32,24},{40,32},{48,40},{56,48},{1,57}... | collective-permute-start | bytes 393224 | tf_op jit(solution)/shard_map/ppermute | solution.py:283
  52.3 6.7 %collective-permute-start.10 = (bf16[4,4,32,128]{3,2,1,0:T(8,128)(2,1)S(1)}, bf16[4,4,32,128]{3,2,1,0:T(8,128)(2,1)S(1)}, u32[]{:S(2)}, u32[]{:S(2)}) collective-permute-start(bf16[4,4,32,128]{3,2,1,0:T(8,128)(2,1)S(1)} %collective-permute-done.6.refs_8_), channel_id=1, source_target_pairs={{0,8},{8,16},{16,24},{24,32},{32,40},{40,48},{48,56},{56,0},{1,9},... | collective-permute-start | bytes 393224 | tf_op jit(solution)/shard_map/ppermute | solution.py:282
  53.7 6.7 %collective-permute-start.13 = (bf16[4,4,32,128]{3,2,1,0:T(8,128)(2,1)S(1)}, bf16[4,4,32,128]{3,2,1,0:T(8,128)(2,1)S(1)}, u32[]{:S(2)}, u32[]{:S(2)}) collective-permute-start(bf16[4,4,32,128]{3,2,1,0:T(8,128)(2,1)S(1)} %collective-permute-done.9.refs_11_), channel_id=1, source_target_pairs={{0,8},{8,16},{16,24},{24,32},{32,40},{40,48},{48,56},{56,0},{1,9},... | collective-permute-start | bytes 393224 | tf_op jit(solution)/shard_map/ppermute | solution.py:285
  54.2 6.2 %collective-permute-start.14 = (bf16[4,4,32,128]{3,2,1,0:T(8,128)(2,1)S(1)}, bf16[4,4,32,128]{3,2,1,0:T(8,128)(2,1)S(1)}, u32[]{:S(2)}, u32[]{:S(2)}) collective-permute-start(bf16[4,4,32,128]{3,2,1,0:T(8,128)(2,1)S(1)} %collective-permute-done.12.refs_14_), channel_id=1, source_target_pairs={{0,56},{8,0},{16,8},{24,16},{32,24},{40,32},{48,40},{56,48},{1,57}... | collective-permute-start | bytes 393224 | tf_op jit(solution)/shard_map/ppermute | solution.py:286
  63.2 14.0 %collective-permute-start.15 = (bf16[2,128,512]{2,1,0:T(8,128)(2,1)S(1)}, bf16[2,128,512]{2,1,0:T(8,128)(2,1)S(1)}, u32[]{:S(2)}, u32[]{:S(2)}) collective-permute-start(bf16[2,128,512]{2,1,0:T(8,128)(2,1)S(1)} %get-tuple-element.17), channel_id=1, source_target_pairs={{0,6},{1,7},{2,4},{3,5},{4,2},{5,3},{6,0},{7,1},{8,14},{9,15},{10,... | collective-permute-start | bytes 786440 | tf_op jit(solution)/shard_map/ppermute | solution.py:314
  64.8 19.7 %collective-permute-start.16 = (bf16[2,128,512]{2,1,0:T(8,128)(2,1)S(1)}, bf16[2,128,512]{2,1,0:T(8,128)(2,1)S(1)}, u32[]{:S(2)}, u32[]{:S(2)}) collective-permute-start(bf16[2,128,512]{2,1,0:T(8,128)(2,1)S(1)} %get-tuple-element.18), channel_id=1, source_target_pairs={{0,2},{1,3},{2,0},{3,1},{4,6},{5,7},{6,4},{7,5},{8,10},{9,11},{10,... | collective-permute-start | bytes 786440 | tf_op jit(solution)/shard_map/ppermute | solution.py:314
  67.6 19.4 %collective-permute-start.17 = (bf16[2,128,512]{2,1,0:T(8,128)(2,1)}, bf16[2,128,512]{2,1,0:T(8,128)(2,1)S(1)}, u32[]{:S(2)}, u32[]{:S(2)}) collective-permute-start(bf16[2,128,512]{2,1,0:T(8,128)(2,1)} %get-tuple-element.19), channel_id=1, source_target_pairs={{0,5},{1,6},{2,7},{3,4},{4,1},{5,2},{6,3},{7,0},{8,13},{9,14},{10,... | collective-permute-start | bytes 786440 | tf_op jit(solution)/shard_map/ppermute | solution.py:314
  70.1 16.9 %collective-permute-start.18 = (bf16[2,128,512]{2,1,0:T(8,128)(2,1)S(1)}, bf16[2,128,512]{2,1,0:T(8,128)(2,1)S(1)}, u32[]{:S(2)}, u32[]{:S(2)}) collective-permute-start(bf16[2,128,512]{2,1,0:T(8,128)(2,1)S(1)} %get-tuple-element.20), channel_id=1, source_target_pairs={{0,7},{1,4},{2,5},{3,6},{4,3},{5,0},{6,1},{7,2},{8,15},{9,12},{10,... | collective-permute-start | bytes 786440 | tf_op jit(solution)/shard_map/ppermute | solution.py:314
  73.2 15.9 %collective-permute-start.19 = (bf16[2,128,512]{2,1,0:T(8,128)(2,1)S(1)}, bf16[2,128,512]{2,1,0:T(8,128)(2,1)S(1)}, u32[]{:S(2)}, u32[]{:S(2)}) collective-permute-start(bf16[2,128,512]{2,1,0:T(8,128)(2,1)S(1)} %get-tuple-element.21), channel_id=1, source_target_pairs={{0,1},{1,2},{2,3},{3,0},{4,5},{5,6},{6,7},{7,4},{8,9},{9,10},{10,1... | collective-permute-start | bytes 786440 | tf_op jit(solution)/shard_map/ppermute | solution.py:314
  77.2 12.0 %collective-permute-start.20 = (bf16[2,128,512]{2,1,0:T(8,128)(2,1)S(1)}, bf16[2,128,512]{2,1,0:T(8,128)(2,1)S(1)}, u32[]{:S(2)}, u32[]{:S(2)}) collective-permute-start(bf16[2,128,512]{2,1,0:T(8,128)(2,1)S(1)} %get-tuple-element.22), channel_id=1, source_target_pairs={{0,3},{1,0},{2,1},{3,2},{4,7},{5,4},{6,5},{7,6},{8,11},{9,8},{10,9... | collective-permute-start | bytes 786440 | tf_op jit(solution)/shard_map/ppermute | solution.py:314
  84.5 7.9 %collective-permute-start.21 = (bf16[2,128,512]{2,1,0:T(8,128)(2,1)S(1)}, bf16[2,128,512]{2,1,0:T(8,128)(2,1)S(1)}, u32[]{:S(2)}, u32[]{:S(2)}) collective-permute-start(bf16[2,128,512]{2,1,0:T(8,128)(2,1)S(1)} %get-tuple-element.23), channel_id=1, source_target_pairs={{0,4},{1,5},{2,6},{3,7},{4,0},{5,1},{6,2},{7,3},{8,12},{9,13},{10,... | collective-permute-start | bytes 786440 | tf_op jit(solution)/shard_map/ppermute | solution.py:314

commit v2 on v1

v2 whole, which is shorter than its diff:
```python
import math

import jax
import jax.numpy as jnp
import numpy as np
from jax import lax
from jax.experimental import pallas as pl
from jax.experimental.pallas import tpu as pltpu
from jax.sharding import Mesh
from jax.sharding import PartitionSpec as P

NFFT = 2048
TAPS = 4
NSEL = 32
LANES = 128
MIB = 1 << 20


def shifted(count, distance):
    return [(i, (i + distance) % count) for i in range(count)]


def filter_taps():
    position = (
        lax.broadcasted_iota(jnp.int32, (8, NFFT), 0) * NFFT
        + lax.broadcasted_iota(jnp.int32, (8, NFFT), 1)
    ).astype(jnp.float32) + 0.5
    turn = math.pi * (position / NFFT - TAPS / 2.0)
    hann_part = 0.5 - 0.5 * jnp.cos(2.0 * math.pi * position / (TAPS * NFFT))
    return jnp.sin(turn) / turn * hann_part


def signed_angle(phase):
    folded = ((phase + NFFT // 2) & (NFFT - 1)) - NFFT // 2
    return folded.astype(jnp.float32) * (2.0 * math.pi / NFFT)


def table_kernel(order, sel_hbm, volt_ref, table_ref, spill_ref, held_ref, sel_ref, sems):
    chunks = sems.shape[0] - 1
    fetch = pltpu.make_async_copy(sel_hbm, sel_ref, sems.at[chunks])
    fetch.start()
    width = volt_ref.shape[2] // chunks
    copies = []
    for c in reversed(range(chunks)):
        part = pl.ds(c * width, width)
        copy = pltpu.make_async_copy(volt_ref.at[:, :, part], held_ref.at[:, :, part], sems.at[c])
        copy.start()
        copies.append(copy)
    window = filter_taps().T
    fetch.wait()
    lane = lax.broadcasted_iota(jnp.int32, (1, LANES), 1)
    slot = lane & (NSEL - 1)
    sel = jnp.zeros((1, LANES), jnp.int32)
    for position, channel in enumerate(order):
        sel = jnp.where(slot == position, sel_ref[channel], sel)
    quarter = jnp.where((lane & NSEL) != 0, NFFT // 4, 0)
    coarse = lax.broadcasted_iota(jnp.int32, (32, LANES), 0) * 64
    fine = lax.broadcasted_iota(jnp.int32, (64, LANES), 0)
    coarse_angle = signed_angle(coarse * sel)
    fine_angle = signed_angle(fine * sel + quarter)
    coarse_cos, coarse_sin = jnp.cos(coarse_angle), jnp.sin(coarse_angle)
    fine_cos, fine_sin = jnp.cos(fine_angle), jnp.sin(fine_angle)
    upper_lane = lax.broadcasted_iota(jnp.int32, (64, LANES), 1) < LANES // 2
    for a in range(32):
        wave = coarse_cos[a : a + 1, :] * fine_cos - coarse_sin[a : a + 1, :] * fine_sin
        rows = slice(64 * a, 64 * (a + 1))
        for tap in range(TAPS):
            exact = window[rows, tap : tap + 1] * wave
            upper = exact.astype(jnp.bfloat16).astype(jnp.float32)
            table_ref[rows, LANES * tap : LANES * (tap + 1)] = jnp.where(
                upper_lane, upper, exact - upper
            ).astype(jnp.bfloat16)
    copies[0].wait()
    inputs = held_ref.shape[1]
    frames = held_ref.shape[2] // NFFT
    tail = range(frames - TAPS + 1, frames)
    product = jnp.dot(
        jnp.concatenate([held_ref[0, :, NFFT * f : NFFT * (f + 1)] for f in tail], axis=0),
        table_ref[...],
        preferred_element_type=jnp.float32,
    )
    for spectrum in range(TAPS - 1):
        total = jnp.zeros((inputs, LANES), jnp.float32)
        for f in range(spectrum, TAPS - 1):
            tap = f - spectrum
            total += product[inputs * f : inputs * (f + 1), LANES * tap : LANES * (tap + 1)]
        spill_ref[inputs * spectrum : inputs * (spectrum + 1), :] = total
    for copy in copies[1:]:
        copy.wait()


def filter_kernel(batch, volt_ref, table_ref, out_ref):
    inputs = volt_ref.shape[1]
    frames = volt_ref.shape[2] // NFFT
    reach = (TAPS - 1) * inputs
    rows = batch * inputs
    out_ref[...] = jnp.zeros_like(out_ref)
    for first in range(0, frames, batch):
        stacked = jnp.concatenate(
            [volt_ref[0, :, NFFT * f : NFFT * (f + 1)] for f in range(first, first + batch)], axis=0
        )
        product = jnp.dot(stacked, table_ref[...], preferred_element_type=jnp.float32)
        for tap in range(TAPS):
            start = first * inputs + reach - tap * inputs
            out_ref[start : start + rows, :] += product[:, LANES * tap : LANES * (tap + 1)]


def turn_kernel(spectra, total_ref, halo_ref, out_ref, joined, turned):
    inputs = out_ref.shape[1]
    factor = 1.0 / (24.0 * math.sqrt(NFFT))
    halo_rows = halo_ref.shape[0]
    head = total_ref[0:halo_rows, :] + halo_ref[...]
    body = total_ref[halo_rows : spectra * inputs, :]
    joined[0:halo_rows, :] = (head + pltpu.roll(head, LANES // 2, 1)) * factor
    joined[halo_rows : spectra * inputs, :] = (body + pltpu.roll(body, LANES // 2, 1)) * factor
    low_lane = lax.broadcasted_iota(jnp.int32, (NSEL, LANES), 1) < LANES // 2
    for i in range(0, inputs, 2):
        pair = jnp.concatenate(
            [
                joined[pl.ds(i, spectra, stride=inputs), :],
                joined[pl.ds(i + 1, spectra, stride=inputs), :],
            ],
            axis=0,
        )
        flipped = pair.T
        real, imag = flipped[0:NSEL, :], flipped[NSEL : 2 * NSEL, :]
        turned[pl.ds(i, NSEL, stride=inputs), :] = jnp.where(
            low_lane, real, pltpu.roll(imag, LANES // 2, 1)
        )
        turned[pl.ds(i + 1, NSEL, stride=inputs), :] = jnp.where(
            low_lane, pltpu.roll(real, LANES // 2, 1), imag
        )

    out_ref[...] = turned[...].reshape(NSEL, inputs, LANES).astype(jnp.bfloat16)


def matrix(refs):
    groups, segments = refs[0].shape[:2]
    return jnp.concatenate(
        [
            jnp.concatenate([ref[g, t] for ref in refs for g in range(groups)], axis=0)
            for t in range(segments)
        ],
        axis=1,
    )


def own_rows(refs):
    own = matrix(refs)
    low_lane = lax.broadcasted_iota(jnp.int32, (own.shape[0], LANES), 1) < LANES // 2
    swapped = []
    for start in range(0, own.shape[1], LANES):
        rolled = pltpu.roll(own[:, start : start + LANES].astype(jnp.float32), LANES // 2, 1)
        swapped.append(jnp.where(low_lane, rolled, -rolled).astype(jnp.bfloat16))
    return jnp.concatenate([own, jnp.concatenate(swapped, axis=1)], axis=0)


def tile_of(left, refs, scale):
    tile = lax.dot_general(
        left, matrix(refs), (((1,), (1,)), ((), ())), preferred_element_type=jnp.float32
    )
    return (tile * scale).astype(jnp.bfloat16)


def near_kernel(scale, ring, offsets, split, here_ref, *refs):
    units, products_ref, left_ref = refs[:-2], refs[-2], refs[-1]
    planes = products_ref.shape[0] // 2
    left_ref[...] = own_rows(units[: split[0]])
    span = left_ref.shape[0] // 2
    rows = span // 2
    taken = 0
    for offset, count in zip(offsets, split, strict=True):
        tile = tile_of(left_ref[...], units[taken : taken + count], scale)
        taken += count
        origin = lax.rem(here_ref[0] + offset + ring, ring)
        column = pl.multiple_of(origin % 2 * span, span)
        for side in range(2):
            for part in range(2):
                start = span * part + rows * side
                products_ref[planes * side + origin // 2, part, :, pl.ds(column, span)] = tile[
                    start : start + rows, :
                ]


def far_kernel(scale, ring, reach, count, here_ref, products_ref, left_ref, *refs):
    units, out_refs = refs[:count], refs[count:]
    planes = products_ref.shape[0] // 2
    tile = tile_of(left_ref[...], units, scale)
    span = left_ref.shape[0] // 2
    rows = span // 2
    origin = lax.rem(here_ref[0] + ring // 2, ring)
    column = pl.multiple_of(origin % 2 * span, span)
    for (dx, dy), out_ref in zip(reach, out_refs, strict=True):
        side, plane = lax.rem(here_ref[1] + dx, 2), lax.rem(here_ref[2] + dy, planes)
        out_ref[...] = products_ref[planes * side + plane]

        @pl.when(plane == origin // 2)
        def _(side=side, out_ref=out_ref):
            for part in range(2):
                upper = tile[span * part : span * part + rows, :]
                lower = tile[span * part + rows : span * (part + 1), :]
                out_ref[part, :, pl.ds(column, span)] = jnp.where(side == 0, upper, lower)


def store_kernel(reach, here_ref, *refs):
    count = len(reach)
    pieces, out_ref, wide, sems = refs[:count], refs[-3], refs[-2], refs[-1]
    copies = []
    for k, (dx, dy) in enumerate(reach):
        channel = 4 * lax.rem(here_ref[1] + 2 - dx, 2) + lax.rem(here_ref[2] + 4 - dy, 4)
        for part in range(2):
            wide[k, part] = pieces[k][part].astype(jnp.float32)
            copy = pltpu.make_async_copy(
                wide.at[k, part], out_ref.at[part, channel], sems.at[k, part]
            )
            copy.start()
            copies.append(copy)
    for copy in copies:
        copy.wait()


def vmem(count=1):
    return [pl.BlockSpec(memory_space=pltpu.VMEM)] * count


def smem():
    return pl.BlockSpec(memory_space=pltpu.SMEM)


def body(voltages, selected):
    inputs = voltages.shape[1]
    spectra = voltages.shape[2] // NFFT
    segments = lax.axis_size("y")
    sides = lax.axis_size("xhi")
    ring = lax.axis_size("z")
    here = jnp.stack([lax.axis_index(a) for a in ("z", "xhi", "y")]).astype(jnp.int32)
    here, selected = lax.optimization_barrier((here, selected))

    order = np.arange(NSEL).reshape(2, 2, 2, 4).transpose(2, 0, 1, 3).reshape(-1)
    tables, spill, held = pl.pallas_call(
        lambda *refs: table_kernel([int(c) for c in order], *refs),
        in_specs=[pl.BlockSpec(memory_space=pl.ANY)] * 2,
        out_specs=vmem(3),
        out_shape=[
            jax.ShapeDtypeStruct((NFFT, TAPS * LANES), jnp.bfloat16),
            jax.ShapeDtypeStruct(((TAPS - 1) * inputs, LANES), jnp.float32),
            jax.ShapeDtypeStruct(voltages.shape, voltages.dtype),
        ],
        scratch_shapes=[
            pltpu.SMEM((NSEL,), jnp.int32),
            pltpu.SemaphoreType.DMA((9,)),
        ],
        compiler_params=pltpu.CompilerParams(vmem_limit_bytes=40 * MIB),
        name="tables",
    )(selected, voltages)
    halo = lax.ppermute(spill, "y", [(i, i + 1) for i in range(segments - 1)])

    filtered = pl.pallas_call(
        lambda *refs: filter_kernel(16, *refs),
        in_specs=vmem(2),
        out_specs=vmem()[0],
        out_shape=jax.ShapeDtypeStruct(((spectra + TAPS - 1) * inputs, LANES), jnp.float32),
        compiler_params=pltpu.CompilerParams(vmem_limit_bytes=20 * MIB),
        cost_estimate=pl.CostEstimate(
            flops=2 * spectra * inputs * NFFT * TAPS * LANES,
            bytes_accessed=12 * MIB,
            transcendentals=0,
        ),
        name="filter_bank",
    )(held, tables)

    spectrum = pl.pallas_call(
        lambda *refs: turn_kernel(spectra, *refs),
        in_specs=vmem(2),
        out_specs=vmem()[0],
        out_shape=jax.ShapeDtypeStruct((NSEL, inputs, LANES), jnp.bfloat16),
        scratch_shapes=[
            pltpu.VMEM((spectra * inputs, LANES), jnp.float32),
            pltpu.VMEM((NSEL * inputs, LANES), jnp.float32),
        ],
        compiler_params=pltpu.CompilerParams(vmem_limit_bytes=8 * MIB),
        name="turn",
    )(filtered, halo)

    arrived = lax.all_to_all(
        spectrum, ("xhi", "xlo", "core", "y"), split_axis=0, concat_axis=0, tiled=True
    )
    own = arrived.reshape(8, segments, inputs, LANES)

    half = own.shape[0] // 2
    low, high = own[:half], own[half:]
    near = [low, high]
    right_low = left_low = low
    right_high = left_high = high
    offsets = [0]
    for step in range(1, ring // 2):
        right_low = lax.ppermute(right_low, "z", shifted(ring, 1))
        left_high = lax.ppermute(left_high, "z", shifted(ring, -1))
        right_high = lax.ppermute(right_high, "z", shifted(ring, 1))
        left_low = lax.ppermute(left_low, "z", shifted(ring, -1))
        near += [right_low, right_high, left_low, left_high]
        offsets += [-step, step]
    split = (2,) * len(offsets)
    far = [
        lax.ppermute(right_low, "z", shifted(ring, 1)),
        lax.ppermute(left_high, "z", shifted(ring, -1)),
    ]
    scale = 1.0 / (spectra * segments)
    rows = half * inputs
    reach = ((1, 2), (0, 2), (1, 1), (1, 3), (0, 1), (0, 3), (1, 0), (0, 0))
    piece = jax.ShapeDtypeStruct((2, rows, 4 * rows), jnp.bfloat16)
    products, left = pl.pallas_call(
        lambda *refs: near_kernel(scale, ring, offsets, split, *refs),
        in_specs=[smem()] + vmem(len(near)),
        out_specs=vmem(2),
        out_shape=[
            jax.ShapeDtypeStruct((len(reach), *piece.shape), jnp.bfloat16),
            jax.ShapeDtypeStruct((4 * rows, segments * LANES), jnp.bfloat16),
        ],
        compiler_params=pltpu.CompilerParams(vmem_limit_bytes=10 * MIB),
        cost_estimate=pl.CostEstimate(
            flops=2 * len(offsets) * 4 * rows * 2 * rows * segments * LANES,
            bytes_accessed=4 * MIB,
            transcendentals=0,
        ),
        name="near",
    )(here, *near)
    shares = pl.pallas_call(
        lambda *refs: far_kernel(scale, ring, reach, len(far), *refs),
        in_specs=[smem()] + vmem(2 + len(far)),
        out_specs=vmem(len(reach)),
        out_shape=[piece] * len(reach),
        compiler_params=pltpu.CompilerParams(vmem_limit_bytes=10 * MIB),
        name="far",
    )(here, products, left, *far)
    pieces = []
    for (dx, dy), share in zip(reach, shares, strict=True):
        if dx or dy:
            route = [
                (x * segments + y, (x + dx) % sides * segments + (y + dy) % segments)
                for x in range(sides)
                for y in range(segments)
            ]
            share = lax.ppermute(share, ("xhi", "y"), route)
        pieces.append(share)

    def store(numbers, before):
        return pl.pallas_call(
            lambda *refs: store_kernel([reach[k] for k in numbers], *refs),
            in_specs=[smem()]
            + vmem(len(numbers))
            + [pl.BlockSpec(memory_space=pl.ANY)] * len(before),
            out_specs=pl.BlockSpec(memory_space=pl.ANY),
            out_shape=jax.ShapeDtypeStruct((2, len(reach), rows, 4 * rows), jnp.float32),
            scratch_shapes=[
                pltpu.VMEM((len(numbers), 2, rows, 4 * rows), jnp.float32),
                pltpu.SemaphoreType.DMA((len(numbers), 2)),
            ],
            input_output_aliases={1 + len(numbers): 0} if before else {},
            compiler_params=pltpu.CompilerParams(vmem_limit_bytes=10 * MIB),
            name="store",
        )(here, *[pieces[k] for k in numbers], *before)

    return store((4, 5, 6), (store((7, 0, 1, 2, 3), ()),))


def solution(mesh):
    fine = Mesh(mesh.devices.reshape(2, 2, 8, 2, 4), ("xlo", "core", "z", "xhi", "y"))
    return jax.shard_map(
        body,
        mesh=fine,
        in_specs=(P(("z", "xhi"), ("xlo", "core"), "y"), P()),
        out_specs=P(None, ("xlo", "core"), ("z", "xhi"), "y"),
        check_vma=False,
    )
```

time: 96.2 us -> 91.8 us (0.954)
  waiting for transfers between devices: 24.1 us -> 18.7 us
  starting transfers between devices: 39.1 us -> 40.9 us
    ppermute x9, waiting for transfers between devices: 18.1 us -> 12.6 us  [the longest x7 12.6 us: body(): share = lax.ppermute(share, ('xhi', 'y'), route)]
    ppermute x9, starting transfers between devices: 16.1 us -> 17.9 us  [the longest x7 14.2 us: body(): share = lax.ppermute(share, ('xhi', 'y'), route)]
    pallas_call x1, Pallas kernels: 2.48 us -> 3.49 us  [body(): pl.pallas_call(lambda *refs: table_kernel([int(c) for c in order], *refs)...]
    pallas_call x3 -> x5, Pallas kernels: 12.1 us -> 11.2 us  [the longest x1 4.49 us: body(): pl.pallas_call(lambda *refs: filter_kernel(16, *refs), in_specs=vmem(2),...]
  transfers between devices with their start and end apart: 22 -> 22, of which waited for: 12 -> 10; matrix products, arithmetic and copies ran while one was open for 0% -> 0% of each run, Pallas kernels for 7% -> 9%
where the time goes in v2:
time: 91.8 us; the launch traced here: 91.6 us
  starting transfers between devices  40.9 us (45%)
  waiting for transfers between devices  18.7 us (20%)
  Pallas kernels  16 us (17%)
  blocking collectives  15 us (16%)
    all_to_all x1, blocking collectives, body(): lax.all_to_all(spectrum, ('xhi', 'xlo', 'core', 'y'), split_axis=0, conca...  15 us
    ppermute x7, starting transfers between devices, body(): share = lax.ppermute(share, ('xhi', 'y'), route)  14.2 us
    ppermute x7, waiting for transfers between devices, body(): share = lax.ppermute(share, ('xhi', 'y'), route)  12.6 us
    ppermute x3, starting transfers between devices, body(): left_high = lax.ppermute(left_high, 'z', shifted(ring, -1))  11.4 us
    ppermute x3, starting transfers between devices, body(): left_low = lax.ppermute(left_low, 'z', shifted(ring, -1))  5.58 us
    pallas_call x1, Pallas kernels, body(): pl.pallas_call(lambda *refs: filter_kernel(16, *refs), in_specs=vmem(2),...  4.49 us
    ppermute x3, waiting for transfers between devices, body(): right_low = lax.ppermute(right_low, 'z', shifted(ring, 1))  4.02 us
    pallas_call x2, Pallas kernels, store(): pl.pallas_call(lambda *refs: store_kernel([reach[k] for k in numbers], *r...  3.86 us
  transfers between devices with their start and end apart: 22, of which 10 were waited for; matrix products, arithmetic and copies ran while one was open for 0% of the time, Pallas kernels for 9%

profile of v2, /device:TPU:2, one launch (start us, length us, event | category | flops | bytes accessed | tf_op | source)
XLA Modules:
  0.0 91.6 jit_solution(10800345784861389659)
XLA Ops:
  0.0 0.1 pad_add_fusion.refs_0_
  0.1 0.0 copy-start
  0.1 0.7 copy-done
  0.7 3.5 %tables.1 = (bf16[2048,512]{1,0:T(8,128)(2,1)S(1)}, f32[96,128]{1,0:T(8,128)S(1)}, bf16[1,32,131072]{2,1,0:T(8,128)(2,1)S(1)}) custom-call(s32[32]{0:T(128)S(1)} %copy-done, bf16[1,32,131072]{2,1,0:T(8,128)(2,1)} %refs_1_.1), custom_call_target="tpu_custom_call" | custom-call | tf_op jit(solution)/shard_map/tables/pallas_call | solution.py:240
  4.2 3.5 %collective-permute-start = (f32[96,128]{1,0:T(8,128)S(1)}, f32[96,128]{1,0:T(8,128)S(1)}, u32[]{:S(2)}, u32[]{:S(2)}) collective-permute-start(f32[96,128]{1,0:T(8,128)S(1)} %get-tuple-element.24), channel_id=1, source_target_pairs={{0,1},{1,2},{2,3},{4,5},{5,6},{6,7},{8,9},{9,10},{10,11},{12,13},{... | collective-permute-start | bytes 147464 | tf_op jit(solution)/shard_map/ppermute | solution.py:256
  7.7 4.5 %filter_bank.1.refs_0_ = f32[2144,128]{1,0:T(8,128)S(1)} custom-call(bf16[1,32,131072]{2,1,0:T(8,128)(2,1)S(1)} %get-tuple-element.22.refs_0_, bf16[2048,512]{1,0:T(8,128)(2,1)S(1)} %get-tuple-element.23.refs_1_), custom_call_target="tpu_custom_call" | custom-call | flops 4294967296 | bytes 12582912 | tf_op jit(solution)/shard_map/filter_bank/pallas_call | solution.py:258
  12.2 0.0 collective-permute-done.refs_1_
  12.2 1.4 %turn.1 = bf16[32,32,128]{2,1,0:T(8,128)(2,1)S(1)} custom-call(f32[2144,128]{1,0:T(8,128)S(1)} %filter_bank.1.refs_0_, f32[96,128]{1,0:T(8,128)S(1)} %collective-permute-done.refs_1_), custom_call_target="tpu_custom_call" | custom-call | tf_op jit(solution)/shard_map/turn/pallas_call | solution.py:272
  13.6 15.0 %all_to_all.5 = bf16[32,32,128]{2,1,0:T(8,128)(2,1)S(1)} all-to-all(bf16[32,32,128]{2,1,0:T(8,128)(2,1)S(1)} %turn.1), channel_id=1, replica_groups=mesh['xlo'=2,'core'=2,'z'=8,'xhi'=2,'y'=4] {'xhi','xlo','core','y'}, dimensions={0} | all-to-all | bytes 524288 | tf_op jit(solution)/shard_map/all_to_all | solution.py:285
  28.7 2.0 %collective-permute-start.1 = (bf16[4,4,32,128]{3,2,1,0:T(8,128)(2,1)S(1)}, bf16[4,4,32,128]{3,2,1,0:T(8,128)(2,1)S(1)}, u32[]{:S(2)}, u32[]{:S(2)}) collective-permute-start(bf16[4,4,32,128]{3,2,1,0:T(8,128)(2,1)S(1)} %bitcast.8), channel_id=1, source_target_pairs={{0,8},{8,16},{16,24},{24,32},{32,40},{40,48},{48,56},{56,0},{1,9},... | collective-permute-start | bytes 393224 | tf_op jit(solution)/shard_map/ppermute | solution.py:297
  30.6 4.0 %collective-permute-start.4 = (bf16[4,4,32,128]{3,2,1,0:T(8,128)(2,1)S(1)}, bf16[4,4,32,128]{3,2,1,0:T(8,128)(2,1)S(1)}, u32[]{:S(2)}, u32[]{:S(2)}) collective-permute-start(bf16[4,4,32,128]{3,2,1,0:T(8,128)(2,1)S(1)} %bitcast.5), channel_id=1, source_target_pairs={{0,56},{8,0},{16,8},{24,16},{32,24},{40,32},{48,40},{56,48},{1,57}... | collective-permute-start | bytes 393224 | tf_op jit(solution)/shard_map/ppermute | solution.py:298
  34.7 1.9 %collective-permute-start.3 = (bf16[4,4,32,128]{3,2,1,0:T(8,128)(2,1)S(1)}, bf16[4,4,32,128]{3,2,1,0:T(8,128)(2,1)S(1)}, u32[]{:S(2)}, u32[]{:S(2)}) collective-permute-start(bf16[4,4,32,128]{3,2,1,0:T(8,128)(2,1)S(1)} %bitcast.9), channel_id=1, source_target_pairs={{0,56},{8,0},{16,8},{24,16},{32,24},{40,32},{48,40},{56,48},{1,57}... | collective-permute-start | bytes 393224 | tf_op jit(solution)/shard_map/ppermute | solution.py:300
  36.6 0.1 collective-permute-start.2
  36.7 1.7 %collective-permute-done.1.refs_3_ = bf16[4,4,32,128]{3,2,1,0:T(8,128)(2,1)S(1)} collective-permute-done((bf16[4,4,32,128]{3,2,1,0:T(8,128)(2,1)S(1)}, bf16[4,4,32,128]{3,2,1,0:T(8,128)(2,1)S(1)}, u32[]{:S(2)}, u32[]{:S(2)}) %collective-permute-start.1) | collective-permute-done | bytes 131104 | tf_op jit(solution)/shard_map/ppermute | solution.py:297
  38.4 0.0 collective-permute-start.5
  38.4 0.2 collective-permute-done.4.refs_6_
  38.5 3.7 %collective-permute-start.8 = (bf16[4,4,32,128]{3,2,1,0:T(8,128)(2,1)S(1)}, bf16[4,4,32,128]{3,2,1,0:T(8,128)(2,1)S(1)}, u32[]{:S(2)}, u32[]{:S(2)}) collective-permute-start(bf16[4,4,32,128]{3,2,1,0:T(8,128)(2,1)S(1)} %collective-permute-done.4.refs_6_), channel_id=1, source_target_pairs={{0,56},{8,0},{16,8},{24,16},{32,24},{40,32},{48,40},{56,48},{1,57}... | collective-permute-start | bytes 393224 | tf_op jit(solution)/shard_map/ppermute | solution.py:298
  42.2 0.0 collective-permute-done.3.refs_5_
  42.2 2.0 %collective-permute-start.7 = (bf16[4,4,32,128]{3,2,1,0:T(8,128)(2,1)S(1)}, bf16[4,4,32,128]{3,2,1,0:T(8,128)(2,1)S(1)}, u32[]{:S(2)}, u32[]{:S(2)}) collective-permute-start(bf16[4,4,32,128]{3,2,1,0:T(8,128)(2,1)S(1)} %collective-permute-done.3.refs_5_), channel_id=1, source_target_pairs={{0,56},{8,0},{16,8},{24,16},{32,24},{40,32},{48,40},{56,48},{1,57}... | collective-permute-start | bytes 393224 | tf_op jit(solution)/shard_map/ppermute | solution.py:300
  44.2 0.0 collective-permute-done.2.refs_4_
  44.2 0.1 collective-permute-start.6
  44.3 1.3 %collective-permute-done.5.refs_7_ = bf16[4,4,32,128]{3,2,1,0:T(8,128)(2,1)S(1)} collective-permute-done((bf16[4,4,32,128]{3,2,1,0:T(8,128)(2,1)S(1)}, bf16[4,4,32,128]{3,2,1,0:T(8,128)(2,1)S(1)}, u32[]{:S(2)}, u32[]{:S(2)}) %collective-permute-start.5) | collective-permute-done | bytes 131104 | tf_op jit(solution)/shard_map/ppermute | solution.py:297
  45.6 0.0 collective-permute-start.9
  45.6 0.2 collective-permute-done.8.refs_10_
  45.9 3.7 %collective-permute-start.12 = (bf16[4,4,32,128]{3,2,1,0:T(8,128)(2,1)S(1)}, bf16[4,4,32,128]{3,2,1,0:T(8,128)(2,1)S(1)}, u32[]{:S(2)}, u32[]{:S(2)}) collective-permute-start(bf16[4,4,32,128]{3,2,1,0:T(8,128)(2,1)S(1)} %collective-permute-done.8.refs_10_), channel_id=1, source_target_pairs={{0,56},{8,0},{16,8},{24,16},{32,24},{40,32},{48,40},{56,48},{1,57}... | collective-permute-start | bytes 393224 | tf_op jit(solution)/shard_map/ppermute | solution.py:298
  49.5 0.0 collective-permute-done.7.refs_9_
  49.6 1.7 %collective-permute-start.11 = (bf16[4,4,32,128]{3,2,1,0:T(8,128)(2,1)S(1)}, bf16[4,4,32,128]{3,2,1,0:T(8,128)(2,1)S(1)}, u32[]{:S(2)}, u32[]{:S(2)}) collective-permute-start(bf16[4,4,32,128]{3,2,1,0:T(8,128)(2,1)S(1)} %collective-permute-done.7.refs_9_), channel_id=1, source_target_pairs={{0,56},{8,0},{16,8},{24,16},{32,24},{40,32},{48,40},{56,48},{1,57}... | collective-permute-start | bytes 393224 | tf_op jit(solution)/shard_map/ppermute | solution.py:300
  51.2 0.0 collective-permute-done.6.refs_8_
  51.2 0.4 collective-permute-start.10
  51.6 1.0 %collective-permute-done.9.refs_11_ = bf16[4,4,32,128]{3,2,1,0:T(8,128)(2,1)S(1)} collective-permute-done((bf16[4,4,32,128]{3,2,1,0:T(8,128)(2,1)S(1)}, bf16[4,4,32,128]{3,2,1,0:T(8,128)(2,1)S(1)}, u32[]{:S(2)}, u32[]{:S(2)}) %collective-permute-start.9) | collective-permute-done | bytes 131104 | tf_op jit(solution)/shard_map/ppermute | solution.py:297
  52.6 0.0 collective-permute-start.13
  52.6 0.5 collective-permute-done.12.refs_14_
  53.1 3.7 %collective-permute-start.14 = (bf16[4,4,32,128]{3,2,1,0:T(8,128)(2,1)S(1)}, bf16[4,4,32,128]{3,2,1,0:T(8,128)(2,1)S(1)}, u32[]{:S(2)}, u32[]{:S(2)}) collective-permute-start(bf16[4,4,32,128]{3,2,1,0:T(8,128)(2,1)S(1)} %collective-permute-done.12.refs_14_), channel_id=1, source_target_pairs={{0,56},{8,0},{16,8},{24,16},{32,24},{40,32},{48,40},{56,48},{1,57}... | collective-permute-start | bytes 393224 | tf_op jit(solution)/shard_map/ppermute | solution.py:306
  56.8 0.0 collective-permute-done.11.refs_13_
  56.8 1.1 %collective-permute-done.10.refs_12_ = bf16[4,4,32,128]{3,2,1,0:T(8,128)(2,1)S(1)} collective-permute-done((bf16[4,4,32,128]{3,2,1,0:T(8,128)(2,1)S(1)}, bf16[4,4,32,128]{3,2,1,0:T(8,128)(2,1)S(1)}, u32[]{:S(2)}, u32[]{:S(2)}) %collective-permute-start.10) | collective-permute-done | bytes 131104 | tf_op jit(solution)/shard_map/ppermute | solution.py:299
  57.9 1.7 %near.1 = (bf16[8,2,128,512]{3,2,1,0:T(8,128)(2,1)S(1)}, bf16[512,512]{1,0:T(8,128)(2,1)S(1)}) custom-call(s32[3]{0:T(128)S(1)} %pad_add_fusion.refs_0_, bf16[4,4,32,128]{3,2,1,0:T(8,128)(2,1)S(1)} %bitcast.10, bf16[4,4,32,128]{3,2,1,0:T(8,128)(2,1)S(1)} %bitcast.7, bf16[4,4,32,128]{3,2,1,0:T(8,128)(2,1)S(1)} %collective-permute-done.1.refs_3_, ...), custom_call_target="tpu_custom_call" | custom-call | flops 939524096 | bytes 4194304 | tf_op jit(solution)/shard_map/near/pallas_call | solution.py:312
  59.7 0.0 collective-permute-done.13.refs_3_
  59.7 0.0 collective-permute-done.14.refs_4_
  59.7 1.1 %far.1 = (bf16[2,128,512]{2,1,0:T(8,128)(2,1)S(1)}, bf16[2,128,512]{2,1,0:T(8,128)(2,1)S(1)}, bf16[2,128,512]{2,1,0:T(8,128)(2,1)S(1)}, bf16[2,128,512]{2,1,0:T(...) custom-call(s32[3]{0:T(128)S(1)} %pad_add_fusion.refs_0_, ...), custom_call_target="tpu_custom_call" | custom-call | tf_op jit(solution)/shard_map/far/pallas_call | solution.py:328
  60.8 1.7 %collective-permute-start.18 = (bf16[2,128,512]{2,1,0:T(8,128)(2,1)S(1)}, bf16[2,128,512]{2,1,0:T(8,128)(2,1)S(1)}, u32[]{:S(2)}, u32[]{:S(2)}) collective-permute-start(bf16[2,128,512]{2,1,0:T(8,128)(2,1)S(1)} %get-tuple-element.31), channel_id=1, source_target_pairs={{0,6},{1,7},{2,4},{3,5},{4,2},{5,3},{6,0},{7,1},{8,14},{9,15},{10,... | collective-permute-start | bytes 786440 | tf_op jit(solution)/shard_map/ppermute | solution.py:344
  62.5 2.8 %collective-permute-start.19 = (bf16[2,128,512]{2,1,0:T(8,128)(2,1)S(1)}, bf16[2,128,512]{2,1,0:T(8,128)(2,1)S(1)}, u32[]{:S(2)}, u32[]{:S(2)}) collective-permute-start(bf16[2,128,512]{2,1,0:T(8,128)(2,1)S(1)} %get-tuple-element.32), channel_id=1, source_target_pairs={{0,2},{1,3},{2,0},{3,1},{4,6},{5,7},{6,4},{7,5},{8,10},{9,11},{10,... | collective-permute-start | bytes 786440 | tf_op jit(solution)/shard_map/ppermute | solution.py:344
  65.3 0.9 collective-permute-start.15
  66.1 1.6 %collective-permute-start.20 = (bf16[2,128,512]{2,1,0:T(8,128)(2,1)S(1)}, bf16[2,128,512]{2,1,0:T(8,128)(2,1)S(1)}, u32[]{:S(2)}, u32[]{:S(2)}) collective-permute-start(bf16[2,128,512]{2,1,0:T(8,128)(2,1)S(1)} %get-tuple-element.33), channel_id=1, source_target_pairs={{0,5},{1,6},{2,7},{3,4},{4,1},{5,2},{6,3},{7,0},{8,13},{9,14},{10,... | collective-permute-start | bytes 786440 | tf_op jit(solution)/shard_map/ppermute | solution.py:344
  67.8 4.0 %collective-permute-start.21 = (bf16[2,128,512]{2,1,0:T(8,128)(2,1)S(1)}, bf16[2,128,512]{2,1,0:T(8,128)(2,1)S(1)}, u32[]{:S(2)}, u32[]{:S(2)}) collective-permute-start(bf16[2,128,512]{2,1,0:T(8,128)(2,1)S(1)} %get-tuple-element.34), channel_id=1, source_target_pairs={{0,7},{1,4},{2,5},{3,6},{4,3},{5,0},{6,1},{7,2},{8,15},{9,12},{10,... | collective-permute-start | bytes 786440 | tf_op jit(solution)/shard_map/ppermute | solution.py:344
  71.8 1.5 %collective-permute-done.18.refs_2_ = bf16[2,128,512]{2,1,0:T(8,128)(2,1)S(1)} collective-permute-done((bf16[2,128,512]{2,1,0:T(8,128)(2,1)S(1)}, bf16[2,128,512]{2,1,0:T(8,128)(2,1)S(1)}, u32[]{:S(2)}, u32[]{:S(2)}) %collective-permute-start.18) | collective-permute-done | bytes 262176 | tf_op jit(solution)/shard_map/ppermute | solution.py:344
  73.3 1.3 %collective-permute-start.16 = (bf16[2,128,512]{2,1,0:T(8,128)(2,1)S(1)}, bf16[2,128,512]{2,1,0:T(8,128)(2,1)S(1)}, u32[]{:S(2)}, u32[]{:S(2)}) collective-permute-start(bf16[2,128,512]{2,1,0:T(8,128)(2,1)S(1)} %get-tuple-element.28), channel_id=1, source_target_pairs={{0,3},{1,0},{2,1},{3,2},{4,7},{5,4},{6,5},{7,6},{8,11},{9,8},{10,9... | collective-permute-start | bytes 786440 | tf_op jit(solution)/shard_map/ppermute | solution.py:344
  74.6 7.3 %collective-permute-done.19.refs_3_ = bf16[2,128,512]{2,1,0:T(8,128)(2,1)S(1)} collective-permute-done((bf16[2,128,512]{2,1,0:T(8,128)(2,1)S(1)}, bf16[2,128,512]{2,1,0:T(8,128)(2,1)S(1)}, u32[]{:S(2)}, u32[]{:S(2)}) %collective-permute-start.19) | collective-permute-done | bytes 262176 | tf_op jit(solution)/shard_map/ppermute | solution.py:344
  81.9 1.9 %collective-permute-start.17 = (bf16[2,128,512]{2,1,0:T(8,128)(2,1)S(1)}, bf16[2,128,512]{2,1,0:T(8,128)(2,1)S(1)}, u32[]{:S(2)}, u32[]{:S(2)}) collective-permute-start(bf16[2,128,512]{2,1,0:T(8,128)(2,1)S(1)} %get-tuple-element.29), channel_id=1, source_target_pairs={{0,4},{1,5},{2,6},{3,7},{4,0},{5,1},{6,2},{7,3},{8,12},{9,13},{10,... | collective-permute-start | bytes 786440 | tf_op jit(solution)/shard_map/ppermute | solution.py:344
  83.8 0.0 collective-permute-done.20.refs_4_
  83.8 0.0 collective-permute-done.21.refs_5_
  83.8 2.1 %store.2.refs_4_ = f32[2,8,128,512]{3,2,1,0:T(8,128)} custom-call(s32[3]{0:T(128)S(1)} %pad_add_fusion.refs_0_, bf16[2,128,512]{2,1,0:T(8,128)(2,1)S(1)} %get-tuple-element.30.refs_1_, bf16[2,128,512]{2,1,0:T(8,128)(2,1)S(1)} %collective-permute-done.18.refs_2_, bf16[2,128,512]{2,1,0:T(8,128)(2,1)S(1)} %collective-permute-done.19.refs_3_, ...), custom_call_target="tpu_custom_call" | custom-call | tf_op jit(solution)/shard_map/store/pallas_call | solution.py:348
  85.9 0.0 collective-permute-done.15.refs_1_
  85.9 0.0 collective-permute-done.16.refs_2_
  86.0 3.8 %collective-permute-done.17.refs_3_ = bf16[2,128,512]{2,1,0:T(8,128)(2,1)S(1)} collective-permute-done((bf16[2,128,512]{2,1,0:T(8,128)(2,1)S(1)}, bf16[2,128,512]{2,1,0:T(8,128)(2,1)S(1)}, u32[]{:S(2)}, u32[]{:S(2)}) %collective-permute-start.17) | collective-permute-done | bytes 262176 | tf_op jit(solution)/shard_map/ppermute | solution.py:344
  89.7 1.7 %store.3 = f32[2,8,128,512]{3,2,1,0:T(8,128)} custom-call(s32[3]{0:T(128)S(1)} %pad_add_fusion.refs_0_, bf16[2,128,512]{2,1,0:T(8,128)(2,1)S(1)} %collective-permute-done.15.refs_1_, bf16[2,128,512]{2,1,0:T(8,128)(2,1)S(1)} %collective-permute-done.16.refs_2_, ...), custom_call_target="tpu_custom_call", output_to_operand_aliasing={{}: (4, {})} | custom-call | tf_op jit(solution)/shard_map/store/pallas_call | solution.py:348
  (1 shorter events, 0.0 us)
Async XLA Ops:
  0.1 0.7 copy-start
  4.2 8.0 %collective-permute-start = (f32[96,128]{1,0:T(8,128)S(1)}, f32[96,128]{1,0:T(8,128)S(1)}, u32[]{:S(2)}, u32[]{:S(2)}) collective-permute-start(f32[96,128]{1,0:T(8,128)S(1)} %get-tuple-element.24), channel_id=1, source_target_pairs={{0,1},{1,2},{2,3},{4,5},{5,6},{6,7},{8,9},{9,10},{10,11},{12,13},{... | collective-permute-start | bytes 147464 | tf_op jit(solution)/shard_map/ppermute | solution.py:256
  28.7 9.7 %collective-permute-start.1 = (bf16[4,4,32,128]{3,2,1,0:T(8,128)(2,1)S(1)}, bf16[4,4,32,128]{3,2,1,0:T(8,128)(2,1)S(1)}, u32[]{:S(2)}, u32[]{:S(2)}) collective-permute-start(bf16[4,4,32,128]{3,2,1,0:T(8,128)(2,1)S(1)} %bitcast.8), channel_id=1, source_target_pairs={{0,8},{8,16},{16,24},{24,32},{32,40},{40,48},{48,56},{56,0},{1,9},... | collective-permute-start | bytes 393224 | tf_op jit(solution)/shard_map/ppermute | solution.py:297
  30.6 7.9 %collective-permute-start.4 = (bf16[4,4,32,128]{3,2,1,0:T(8,128)(2,1)S(1)}, bf16[4,4,32,128]{3,2,1,0:T(8,128)(2,1)S(1)}, u32[]{:S(2)}, u32[]{:S(2)}) collective-permute-start(bf16[4,4,32,128]{3,2,1,0:T(8,128)(2,1)S(1)} %bitcast.5), channel_id=1, source_target_pairs={{0,56},{8,0},{16,8},{24,16},{32,24},{40,32},{48,40},{56,48},{1,57}... | collective-permute-start | bytes 393224 | tf_op jit(solution)/shard_map/ppermute | solution.py:298
  34.7 7.6 %collective-permute-start.3 = (bf16[4,4,32,128]{3,2,1,0:T(8,128)(2,1)S(1)}, bf16[4,4,32,128]{3,2,1,0:T(8,128)(2,1)S(1)}, u32[]{:S(2)}, u32[]{:S(2)}) collective-permute-start(bf16[4,4,32,128]{3,2,1,0:T(8,128)(2,1)S(1)} %bitcast.9), channel_id=1, source_target_pairs={{0,56},{8,0},{16,8},{24,16},{32,24},{40,32},{48,40},{56,48},{1,57}... | collective-permute-start | bytes 393224 | tf_op jit(solution)/shard_map/ppermute | solution.py:300
  36.6 7.6 %collective-permute-start.2 = (bf16[4,4,32,128]{3,2,1,0:T(8,128)(2,1)S(1)}, bf16[4,4,32,128]{3,2,1,0:T(8,128)(2,1)S(1)}, u32[]{:S(2)}, u32[]{:S(2)}) collective-permute-start(bf16[4,4,32,128]{3,2,1,0:T(8,128)(2,1)S(1)} %bitcast.6), channel_id=1, source_target_pairs={{0,8},{8,16},{16,24},{24,32},{32,40},{40,48},{48,56},{56,0},{1,9},... | collective-permute-start | bytes 393224 | tf_op jit(solution)/shard_map/ppermute | solution.py:299
  38.4 7.2 %collective-permute-start.5 = (bf16[4,4,32,128]{3,2,1,0:T(8,128)(2,1)S(1)}, bf16[4,4,32,128]{3,2,1,0:T(8,128)(2,1)S(1)}, u32[]{:S(2)}, u32[]{:S(2)}) collective-permute-start(bf16[4,4,32,128]{3,2,1,0:T(8,128)(2,1)S(1)} %collective-permute-done.1.refs_3_), channel_id=1, source_target_pairs={{0,8},{8,16},{16,24},{24,32},{32,40},{40,48},{48,56},{56,0},{1,9},... | collective-permute-start | bytes 393224 | tf_op jit(solution)/shard_map/ppermute | solution.py:297
  38.5 7.3 %collective-permute-start.8 = (bf16[4,4,32,128]{3,2,1,0:T(8,128)(2,1)S(1)}, bf16[4,4,32,128]{3,2,1,0:T(8,128)(2,1)S(1)}, u32[]{:S(2)}, u32[]{:S(2)}) collective-permute-start(bf16[4,4,32,128]{3,2,1,0:T(8,128)(2,1)S(1)} %collective-permute-done.4.refs_6_), channel_id=1, source_target_pairs={{0,56},{8,0},{16,8},{24,16},{32,24},{40,32},{48,40},{56,48},{1,57}... | collective-permute-start | bytes 393224 | tf_op jit(solution)/shard_map/ppermute | solution.py:298
  42.2 7.3 %collective-permute-start.7 = (bf16[4,4,32,128]{3,2,1,0:T(8,128)(2,1)S(1)}, bf16[4,4,32,128]{3,2,1,0:T(8,128)(2,1)S(1)}, u32[]{:S(2)}, u32[]{:S(2)}) collective-permute-start(bf16[4,4,32,128]{3,2,1,0:T(8,128)(2,1)S(1)} %collective-permute-done.3.refs_5_), channel_id=1, source_target_pairs={{0,56},{8,0},{16,8},{24,16},{32,24},{40,32},{48,40},{56,48},{1,57}... | collective-permute-start | bytes 393224 | tf_op jit(solution)/shard_map/ppermute | solution.py:300
  44.2 7.0 %collective-permute-start.6 = (bf16[4,4,32,128]{3,2,1,0:T(8,128)(2,1)S(1)}, bf16[4,4,32,128]{3,2,1,0:T(8,128)(2,1)S(1)}, u32[]{:S(2)}, u32[]{:S(2)}) collective-permute-start(bf16[4,4,32,128]{3,2,1,0:T(8,128)(2,1)S(1)} %collective-permute-done.2.refs_4_), channel_id=1, source_target_pairs={{0,8},{8,16},{16,24},{24,32},{32,40},{40,48},{48,56},{56,0},{1,9},... | collective-permute-start | bytes 393224 | tf_op jit(solution)/shard_map/ppermute | solution.py:299
  45.6 7.0 %collective-permute-start.9 = (bf16[4,4,32,128]{3,2,1,0:T(8,128)(2,1)S(1)}, bf16[4,4,32,128]{3,2,1,0:T(8,128)(2,1)S(1)}, u32[]{:S(2)}, u32[]{:S(2)}) collective-permute-start(bf16[4,4,32,128]{3,2,1,0:T(8,128)(2,1)S(1)} %collective-permute-done.5.refs_7_), channel_id=1, source_target_pairs={{0,8},{8,16},{16,24},{24,32},{32,40},{40,48},{48,56},{56,0},{1,9},... | collective-permute-start | bytes 393224 | tf_op jit(solution)/shard_map/ppermute | solution.py:297
  45.9 7.3 %collective-permute-start.12 = (bf16[4,4,32,128]{3,2,1,0:T(8,128)(2,1)S(1)}, bf16[4,4,32,128]{3,2,1,0:T(8,128)(2,1)S(1)}, u32[]{:S(2)}, u32[]{:S(2)}) collective-permute-start(bf16[4,4,32,128]{3,2,1,0:T(8,128)(2,1)S(1)} %collective-permute-done.8.refs_10_), channel_id=1, source_target_pairs={{0,56},{8,0},{16,8},{24,16},{32,24},{40,32},{48,40},{56,48},{1,57}... | collective-permute-start | bytes 393224 | tf_op jit(solution)/shard_map/ppermute | solution.py:298
  49.6 7.3 %collective-permute-start.11 = (bf16[4,4,32,128]{3,2,1,0:T(8,128)(2,1)S(1)}, bf16[4,4,32,128]{3,2,1,0:T(8,128)(2,1)S(1)}, u32[]{:S(2)}, u32[]{:S(2)}) collective-permute-start(bf16[4,4,32,128]{3,2,1,0:T(8,128)(2,1)S(1)} %collective-permute-done.7.refs_9_), channel_id=1, source_target_pairs={{0,56},{8,0},{16,8},{24,16},{32,24},{40,32},{48,40},{56,48},{1,57}... | collective-permute-start | bytes 393224 | tf_op jit(solution)/shard_map/ppermute | solution.py:300
  51.2 6.7 %collective-permute-start.10 = (bf16[4,4,32,128]{3,2,1,0:T(8,128)(2,1)S(1)}, bf16[4,4,32,128]{3,2,1,0:T(8,128)(2,1)S(1)}, u32[]{:S(2)}, u32[]{:S(2)}) collective-permute-start(bf16[4,4,32,128]{3,2,1,0:T(8,128)(2,1)S(1)} %collective-permute-done.6.refs_8_), channel_id=1, source_target_pairs={{0,8},{8,16},{16,24},{24,32},{32,40},{40,48},{48,56},{56,0},{1,9},... | collective-permute-start | bytes 393224 | tf_op jit(solution)/shard_map/ppermute | solution.py:299
  52.6 7.1 %collective-permute-start.13 = (bf16[4,4,32,128]{3,2,1,0:T(8,128)(2,1)S(1)}, bf16[4,4,32,128]{3,2,1,0:T(8,128)(2,1)S(1)}, u32[]{:S(2)}, u32[]{:S(2)}) collective-permute-start(bf16[4,4,32,128]{3,2,1,0:T(8,128)(2,1)S(1)} %collective-permute-done.9.refs_11_), channel_id=1, source_target_pairs={{0,8},{8,16},{16,24},{24,32},{32,40},{40,48},{48,56},{56,0},{1,9},... | collective-permute-start | bytes 393224 | tf_op jit(solution)/shard_map/ppermute | solution.py:305
  53.1 6.6 %collective-permute-start.14 = (bf16[4,4,32,128]{3,2,1,0:T(8,128)(2,1)S(1)}, bf16[4,4,32,128]{3,2,1,0:T(8,128)(2,1)S(1)}, u32[]{:S(2)}, u32[]{:S(2)}) collective-permute-start(bf16[4,4,32,128]{3,2,1,0:T(8,128)(2,1)S(1)} %collective-permute-done.12.refs_14_), channel_id=1, source_target_pairs={{0,56},{8,0},{16,8},{24,16},{32,24},{40,32},{48,40},{56,48},{1,57}... | collective-permute-start | bytes 393224 | tf_op jit(solution)/shard_map/ppermute | solution.py:306
  60.8 12.5 %collective-permute-start.18 = (bf16[2,128,512]{2,1,0:T(8,128)(2,1)S(1)}, bf16[2,128,512]{2,1,0:T(8,128)(2,1)S(1)}, u32[]{:S(2)}, u32[]{:S(2)}) collective-permute-start(bf16[2,128,512]{2,1,0:T(8,128)(2,1)S(1)} %get-tuple-element.31), channel_id=1, source_target_pairs={{0,6},{1,7},{2,4},{3,5},{4,2},{5,3},{6,0},{7,1},{8,14},{9,15},{10,... | collective-permute-start | bytes 786440 | tf_op jit(solution)/shard_map/ppermute | solution.py:344
  62.5 19.4 %collective-permute-start.19 = (bf16[2,128,512]{2,1,0:T(8,128)(2,1)S(1)}, bf16[2,128,512]{2,1,0:T(8,128)(2,1)S(1)}, u32[]{:S(2)}, u32[]{:S(2)}) collective-permute-start(bf16[2,128,512]{2,1,0:T(8,128)(2,1)S(1)} %get-tuple-element.32), channel_id=1, source_target_pairs={{0,2},{1,3},{2,0},{3,1},{4,6},{5,7},{6,4},{7,5},{8,10},{9,11},{10,... | collective-permute-start | bytes 786440 | tf_op jit(solution)/shard_map/ppermute | solution.py:344
  65.3 20.7 %collective-permute-start.15 = (bf16[2,128,512]{2,1,0:T(8,128)(2,1)S(1)}, bf16[2,128,512]{2,1,0:T(8,128)(2,1)S(1)}, u32[]{:S(2)}, u32[]{:S(2)}) collective-permute-start(bf16[2,128,512]{2,1,0:T(8,128)(2,1)S(1)} %get-tuple-element.27), channel_id=1, source_target_pairs={{0,1},{1,2},{2,3},{3,0},{4,5},{5,6},{6,7},{7,4},{8,9},{9,10},{10,1... | collective-permute-start | bytes 786440 | tf_op jit(solution)/shard_map/ppermute | solution.py:344
  66.1 17.7 %collective-permute-start.20 = (bf16[2,128,512]{2,1,0:T(8,128)(2,1)S(1)}, bf16[2,128,512]{2,1,0:T(8,128)(2,1)S(1)}, u32[]{:S(2)}, u32[]{:S(2)}) collective-permute-start(bf16[2,128,512]{2,1,0:T(8,128)(2,1)S(1)} %get-tuple-element.33), channel_id=1, source_target_pairs={{0,5},{1,6},{2,7},{3,4},{4,1},{5,2},{6,3},{7,0},{8,13},{9,14},{10,... | collective-permute-start | bytes 786440 | tf_op jit(solution)/shard_map/ppermute | solution.py:344
  67.8 16.1 %collective-permute-start.21 = (bf16[2,128,512]{2,1,0:T(8,128)(2,1)S(1)}, bf16[2,128,512]{2,1,0:T(8,128)(2,1)S(1)}, u32[]{:S(2)}, u32[]{:S(2)}) collective-permute-start(bf16[2,128,512]{2,1,0:T(8,128)(2,1)S(1)} %get-tuple-element.34), channel_id=1, source_target_pairs={{0,7},{1,4},{2,5},{3,6},{4,3},{5,0},{6,1},{7,2},{8,15},{9,12},{10,... | collective-permute-start | bytes 786440 | tf_op jit(solution)/shard_map/ppermute | solution.py:344
  73.3 12.6 %collective-permute-start.16 = (bf16[2,128,512]{2,1,0:T(8,128)(2,1)S(1)}, bf16[2,128,512]{2,1,0:T(8,128)(2,1)S(1)}, u32[]{:S(2)}, u32[]{:S(2)}) collective-permute-start(bf16[2,128,512]{2,1,0:T(8,128)(2,1)S(1)} %get-tuple-element.28), channel_id=1, source_target_pairs={{0,3},{1,0},{2,1},{3,2},{4,7},{5,4},{6,5},{7,6},{8,11},{9,8},{10,9... | collective-permute-start | bytes 786440 | tf_op jit(solution)/shard_map/ppermute | solution.py:344
  81.9 7.9 %collective-permute-start.17 = (bf16[2,128,512]{2,1,0:T(8,128)(2,1)S(1)}, bf16[2,128,512]{2,1,0:T(8,128)(2,1)S(1)}, u32[]{:S(2)}, u32[]{:S(2)}) collective-permute-start(bf16[2,128,512]{2,1,0:T(8,128)(2,1)S(1)} %get-tuple-element.29), channel_id=1, source_target_pairs={{0,4},{1,5},{2,6},{3,7},{4,0},{5,1},{6,2},{7,3},{8,12},{9,13},{10,... | collective-permute-start | bytes 786440 | tf_op jit(solution)/shard_map/ppermute | solution.py:344

commit v3 on v2

--- a/solution.py
+++ b/solution.py
@@ -307,7 +307,7 @@
     ]
     scale = 1.0 / (spectra * segments)
     rows = half * inputs
-    reach = ((1, 2), (0, 2), (1, 1), (1, 3), (0, 1), (0, 3), (1, 0), (0, 0))
+    reach = ((1, 2), (1, 1), (1, 3), (0, 2), (1, 0), (0, 1), (0, 3), (0, 0))
     piece = jax.ShapeDtypeStruct((2, rows, 4 * rows), jnp.bfloat16)
     products, left = pl.pallas_call(
         lambda *refs: near_kernel(scale, ring, offsets, split, *refs),
@@ -361,7 +361,9 @@
             name="store",
         )(here, *[pieces[k] for k in numbers], *before)
 
-    return store((4, 5, 6), (store((7, 0, 1, 2, 3), ()),))
+    part = store((7, 0, 1), ())
+    part = store((2, 3, 4), (part,))
+    return store((5, 6), (part,))
 
 
 def solution(mesh):

time: 91.8 us -> 92 us (level); the launches traced: 91.6 us -> 90.8 us
  starting transfers between devices: 40.9 us -> 38.9 us
  Pallas kernels: 16 us -> 17.2 us
    ppermute x7, starting transfers between devices: 14.2 us -> 12.2 us  [body(): share = lax.ppermute(share, ('xhi', 'y'), route)]
    pallas_call x2 -> x3, Pallas kernels: 3.86 us -> 5.04 us  [store(): pl.pallas_call(lambda *refs: store_kernel([reach[k] for k in numbers], *r...]
  transfers between devices with their start and end apart: 22 -> 22, of which waited for: 10 -> 11; matrix products, arithmetic and copies ran while one was open for 0% -> 0% of each run, Pallas kernels for 9% -> 11%
where the time goes in v3:
time: 92 us; the launch traced here: 90.8 us
  starting transfers between devices  38.9 us (42%)
  waiting for transfers between devices  18.7 us (20%)
  Pallas kernels  17.2 us (19%)
  blocking collectives  15 us (16%)
    all_to_all x1, blocking collectives, body(): lax.all_to_all(spectrum, ('xhi', 'xlo', 'core', 'y'), split_axis=0, conca...  15 us
    ppermute x7, waiting for transfers between devices, body(): share = lax.ppermute(share, ('xhi', 'y'), route)  12.6 us
    ppermute x7, starting transfers between devices, body(): share = lax.ppermute(share, ('xhi', 'y'), route)  12.2 us
    ppermute x3, starting transfers between devices, body(): left_high = lax.ppermute(left_high, 'z', shifted(ring, -1))  11.4 us
    ppermute x3, starting transfers between devices, body(): left_low = lax.ppermute(left_low, 'z', shifted(ring, -1))  5.58 us
    pallas_call x3, Pallas kernels, store(): pl.pallas_call(lambda *refs: store_kernel([reach[k] for k in numbers], *r...  5.04 us
    pallas_call x1, Pallas kernels, body(): pl.pallas_call(lambda *refs: filter_kernel(16, *refs), in_specs=vmem(2),...  4.49 us
    ppermute x3, waiting for transfers between devices, body(): right_low = lax.ppermute(right_low, 'z', shifted(ring, 1))  4.02 us
  transfers between devices with their start and end apart: 22, of which 11 were waited for; matrix products, arithmetic and copies ran while one was open for 0% of the time, Pallas kernels for 11%

profile of v3, /device:TPU:2, one launch (start us, length us, event | category | flops | bytes accessed | tf_op | source)
XLA Modules:
  0.0 90.8 jit_solution(13864673484464500581)
XLA Ops:
  0.0 0.1 pad_add_fusion.refs_0_
  0.1 0.0 copy-start
  0.1 0.7 copy-done
  0.7 3.5 %tables.1 = (bf16[2048,512]{1,0:T(8,128)(2,1)S(1)}, f32[96,128]{1,0:T(8,128)S(1)}, bf16[1,32,131072]{2,1,0:T(8,128)(2,1)S(1)}) custom-call(s32[32]{0:T(128)S(1)} %copy-done, bf16[1,32,131072]{2,1,0:T(8,128)(2,1)} %refs_1_.1), custom_call_target="tpu_custom_call" | custom-call | tf_op jit(solution)/shard_map/tables/pallas_call | solution.py:240
  4.2 3.5 %collective-permute-start = (f32[96,128]{1,0:T(8,128)S(1)}, f32[96,128]{1,0:T(8,128)S(1)}, u32[]{:S(2)}, u32[]{:S(2)}) collective-permute-start(f32[96,128]{1,0:T(8,128)S(1)} %get-tuple-element.24), channel_id=1, source_target_pairs={{0,1},{1,2},{2,3},{4,5},{5,6},{6,7},{8,9},{9,10},{10,11},{12,13},{... | collective-permute-start | bytes 147464 | tf_op jit(solution)/shard_map/ppermute | solution.py:256
  7.7 4.5 %filter_bank.1.refs_0_ = f32[2144,128]{1,0:T(8,128)S(1)} custom-call(bf16[1,32,131072]{2,1,0:T(8,128)(2,1)S(1)} %get-tuple-element.22.refs_0_, bf16[2048,512]{1,0:T(8,128)(2,1)S(1)} %get-tuple-element.23.refs_1_), custom_call_target="tpu_custom_call" | custom-call | flops 4294967296 | bytes 12582912 | tf_op jit(solution)/shard_map/filter_bank/pallas_call | solution.py:258
  12.2 0.0 collective-permute-done.refs_1_
  12.2 1.4 %turn.1 = bf16[32,32,128]{2,1,0:T(8,128)(2,1)S(1)} custom-call(f32[2144,128]{1,0:T(8,128)S(1)} %filter_bank.1.refs_0_, f32[96,128]{1,0:T(8,128)S(1)} %collective-permute-done.refs_1_), custom_call_target="tpu_custom_call" | custom-call | tf_op jit(solution)/shard_map/turn/pallas_call | solution.py:272
  13.6 15.0 %all_to_all.5 = bf16[32,32,128]{2,1,0:T(8,128)(2,1)S(1)} all-to-all(bf16[32,32,128]{2,1,0:T(8,128)(2,1)S(1)} %turn.1), channel_id=1, replica_groups=mesh['xlo'=2,'core'=2,'z'=8,'xhi'=2,'y'=4] {'xhi','xlo','core','y'}, dimensions={0} | all-to-all | bytes 524288 | tf_op jit(solution)/shard_map/all_to_all | solution.py:285
  28.7 2.0 %collective-permute-start.1 = (bf16[4,4,32,128]{3,2,1,0:T(8,128)(2,1)S(1)}, bf16[4,4,32,128]{3,2,1,0:T(8,128)(2,1)S(1)}, u32[]{:S(2)}, u32[]{:S(2)}) collective-permute-start(bf16[4,4,32,128]{3,2,1,0:T(8,128)(2,1)S(1)} %bitcast.8), channel_id=1, source_target_pairs={{0,8},{8,16},{16,24},{24,32},{32,40},{40,48},{48,56},{56,0},{1,9},... | collective-permute-start | bytes 393224 | tf_op jit(solution)/shard_map/ppermute | solution.py:297
  30.6 4.0 %collective-permute-start.4 = (bf16[4,4,32,128]{3,2,1,0:T(8,128)(2,1)S(1)}, bf16[4,4,32,128]{3,2,1,0:T(8,128)(2,1)S(1)}, u32[]{:S(2)}, u32[]{:S(2)}) collective-permute-start(bf16[4,4,32,128]{3,2,1,0:T(8,128)(2,1)S(1)} %bitcast.5), channel_id=1, source_target_pairs={{0,56},{8,0},{16,8},{24,16},{32,24},{40,32},{48,40},{56,48},{1,57}... | collective-permute-start | bytes 393224 | tf_op jit(solution)/shard_map/ppermute | solution.py:298
  34.7 1.9 %collective-permute-start.3 = (bf16[4,4,32,128]{3,2,1,0:T(8,128)(2,1)S(1)}, bf16[4,4,32,128]{3,2,1,0:T(8,128)(2,1)S(1)}, u32[]{:S(2)}, u32[]{:S(2)}) collective-permute-start(bf16[4,4,32,128]{3,2,1,0:T(8,128)(2,1)S(1)} %bitcast.9), channel_id=1, source_target_pairs={{0,56},{8,0},{16,8},{24,16},{32,24},{40,32},{48,40},{56,48},{1,57}... | collective-permute-start | bytes 393224 | tf_op jit(solution)/shard_map/ppermute | solution.py:300
  36.6 0.1 collective-permute-start.2
  36.7 1.7 %collective-permute-done.1.refs_3_ = bf16[4,4,32,128]{3,2,1,0:T(8,128)(2,1)S(1)} collective-permute-done((bf16[4,4,32,128]{3,2,1,0:T(8,128)(2,1)S(1)}, bf16[4,4,32,128]{3,2,1,0:T(8,128)(2,1)S(1)}, u32[]{:S(2)}, u32[]{:S(2)}) %collective-permute-start.1) | collective-permute-done | bytes 131104 | tf_op jit(solution)/shard_map/ppermute | solution.py:297
  38.4 0.0 collective-permute-start.5
  38.4 0.2 collective-permute-done.4.refs_6_
  38.5 3.7 %collective-permute-start.8 = (bf16[4,4,32,128]{3,2,1,0:T(8,128)(2,1)S(1)}, bf16[4,4,32,128]{3,2,1,0:T(8,128)(2,1)S(1)}, u32[]{:S(2)}, u32[]{:S(2)}) collective-permute-start(bf16[4,4,32,128]{3,2,1,0:T(8,128)(2,1)S(1)} %collective-permute-done.4.refs_6_), channel_id=1, source_target_pairs={{0,56},{8,0},{16,8},{24,16},{32,24},{40,32},{48,40},{56,48},{1,57}... | collective-permute-start | bytes 393224 | tf_op jit(solution)/shard_map/ppermute | solution.py:298
  42.2 0.0 collective-permute-done.3.refs_5_
  42.2 2.0 %collective-permute-start.7 = (bf16[4,4,32,128]{3,2,1,0:T(8,128)(2,1)S(1)}, bf16[4,4,32,128]{3,2,1,0:T(8,128)(2,1)S(1)}, u32[]{:S(2)}, u32[]{:S(2)}) collective-permute-start(bf16[4,4,32,128]{3,2,1,0:T(8,128)(2,1)S(1)} %collective-permute-done.3.refs_5_), channel_id=1, source_target_pairs={{0,56},{8,0},{16,8},{24,16},{32,24},{40,32},{48,40},{56,48},{1,57}... | collective-permute-start | bytes 393224 | tf_op jit(solution)/shard_map/ppermute | solution.py:300
  44.2 0.0 collective-permute-done.2.refs_4_
  44.2 0.1 collective-permute-start.6
  44.3 1.3 %collective-permute-done.5.refs_7_ = bf16[4,4,32,128]{3,2,1,0:T(8,128)(2,1)S(1)} collective-permute-done((bf16[4,4,32,128]{3,2,1,0:T(8,128)(2,1)S(1)}, bf16[4,4,32,128]{3,2,1,0:T(8,128)(2,1)S(1)}, u32[]{:S(2)}, u32[]{:S(2)}) %collective-permute-start.5) | collective-permute-done | bytes 131104 | tf_op jit(solution)/shard_map/ppermute | solution.py:297
  45.6 0.0 collective-permute-start.9
  45.6 0.2 collective-permute-done.8.refs_10_
  45.9 3.7 %collective-permute-start.12 = (bf16[4,4,32,128]{3,2,1,0:T(8,128)(2,1)S(1)}, bf16[4,4,32,128]{3,2,1,0:T(8,128)(2,1)S(1)}, u32[]{:S(2)}, u32[]{:S(2)}) collective-permute-start(bf16[4,4,32,128]{3,2,1,0:T(8,128)(2,1)S(1)} %collective-permute-done.8.refs_10_), channel_id=1, source_target_pairs={{0,56},{8,0},{16,8},{24,16},{32,24},{40,32},{48,40},{56,48},{1,57}... | collective-permute-start | bytes 393224 | tf_op jit(solution)/shard_map/ppermute | solution.py:298
  49.5 0.0 collective-permute-done.7.refs_9_
  49.6 1.7 %collective-permute-start.11 = (bf16[4,4,32,128]{3,2,1,0:T(8,128)(2,1)S(1)}, bf16[4,4,32,128]{3,2,1,0:T(8,128)(2,1)S(1)}, u32[]{:S(2)}, u32[]{:S(2)}) collective-permute-start(bf16[4,4,32,128]{3,2,1,0:T(8,128)(2,1)S(1)} %collective-permute-done.7.refs_9_), channel_id=1, source_target_pairs={{0,56},{8,0},{16,8},{24,16},{32,24},{40,32},{48,40},{56,48},{1,57}... | collective-permute-start | bytes 393224 | tf_op jit(solution)/shard_map/ppermute | solution.py:300
  51.2 0.0 collective-permute-done.6.refs_8_
  51.2 0.4 collective-permute-start.10
  51.6 1.0 %collective-permute-done.9.refs_11_ = bf16[4,4,32,128]{3,2,1,0:T(8,128)(2,1)S(1)} collective-permute-done((bf16[4,4,32,128]{3,2,1,0:T(8,128)(2,1)S(1)}, bf16[4,4,32,128]{3,2,1,0:T(8,128)(2,1)S(1)}, u32[]{:S(2)}, u32[]{:S(2)}) %collective-permute-start.9) | collective-permute-done | bytes 131104 | tf_op jit(solution)/shard_map/ppermute | solution.py:297
  52.6 0.0 collective-permute-start.13
  52.6 0.5 collective-permute-done.12.refs_14_
  53.1 3.7 %collective-permute-start.14 = (bf16[4,4,32,128]{3,2,1,0:T(8,128)(2,1)S(1)}, bf16[4,4,32,128]{3,2,1,0:T(8,128)(2,1)S(1)}, u32[]{:S(2)}, u32[]{:S(2)}) collective-permute-start(bf16[4,4,32,128]{3,2,1,0:T(8,128)(2,1)S(1)} %collective-permute-done.12.refs_14_), channel_id=1, source_target_pairs={{0,56},{8,0},{16,8},{24,16},{32,24},{40,32},{48,40},{56,48},{1,57}... | collective-permute-start | bytes 393224 | tf_op jit(solution)/shard_map/ppermute | solution.py:306
  56.8 0.0 collective-permute-done.11.refs_13_
  56.8 1.1 %collective-permute-done.10.refs_12_ = bf16[4,4,32,128]{3,2,1,0:T(8,128)(2,1)S(1)} collective-permute-done((bf16[4,4,32,128]{3,2,1,0:T(8,128)(2,1)S(1)}, bf16[4,4,32,128]{3,2,1,0:T(8,128)(2,1)S(1)}, u32[]{:S(2)}, u32[]{:S(2)}) %collective-permute-start.10) | collective-permute-done | bytes 131104 | tf_op jit(solution)/shard_map/ppermute | solution.py:299
  57.9 1.7 %near.1 = (bf16[8,2,128,512]{3,2,1,0:T(8,128)(2,1)S(1)}, bf16[512,512]{1,0:T(8,128)(2,1)S(1)}) custom-call(s32[3]{0:T(128)S(1)} %pad_add_fusion.refs_0_, bf16[4,4,32,128]{3,2,1,0:T(8,128)(2,1)S(1)} %bitcast.10, bf16[4,4,32,128]{3,2,1,0:T(8,128)(2,1)S(1)} %bitcast.7, bf16[4,4,32,128]{3,2,1,0:T(8,128)(2,1)S(1)} %collective-permute-done.1.refs_3_, ...), custom_call_target="tpu_custom_call" | custom-call | flops 939524096 | bytes 4194304 | tf_op jit(solution)/shard_map/near/pallas_call | solution.py:312
  59.7 0.0 collective-permute-done.13.refs_3_
  59.7 0.0 collective-permute-done.14.refs_4_
  59.7 1.1 %far.1 = (bf16[2,128,512]{2,1,0:T(8,128)(2,1)S(1)}, bf16[2,128,512]{2,1,0:T(8,128)(2,1)S(1)}, bf16[2,128,512]{2,1,0:T(8,128)(2,1)S(1)}, bf16[2,128,512]{2,1,0:T(...) custom-call(s32[3]{0:T(128)S(1)} %pad_add_fusion.refs_0_, ...), custom_call_target="tpu_custom_call" | custom-call | tf_op jit(solution)/shard_map/far/pallas_call | solution.py:328
  60.8 1.7 %collective-permute-start.20 = (bf16[2,128,512]{2,1,0:T(8,128)(2,1)S(1)}, bf16[2,128,512]{2,1,0:T(8,128)(2,1)S(1)}, u32[]{:S(2)}, u32[]{:S(2)}) collective-permute-start(bf16[2,128,512]{2,1,0:T(8,128)(2,1)S(1)} %get-tuple-element.33), channel_id=1, source_target_pairs={{0,6},{1,7},{2,4},{3,5},{4,2},{5,3},{6,0},{7,1},{8,14},{9,15},{10,... | collective-permute-start | bytes 786440 | tf_op jit(solution)/shard_map/ppermute | solution.py:344
  62.5 2.4 %collective-permute-start.21 = (bf16[2,128,512]{2,1,0:T(8,128)(2,1)S(1)}, bf16[2,128,512]{2,1,0:T(8,128)(2,1)S(1)}, u32[]{:S(2)}, u32[]{:S(2)}) collective-permute-start(bf16[2,128,512]{2,1,0:T(8,128)(2,1)S(1)} %get-tuple-element.34), channel_id=1, source_target_pairs={{0,5},{1,6},{2,7},{3,4},{4,1},{5,2},{6,3},{7,0},{8,13},{9,14},{10,... | collective-permute-start | bytes 786440 | tf_op jit(solution)/shard_map/ppermute | solution.py:344
  64.9 1.9 %collective-permute-start.15 = (bf16[2,128,512]{2,1,0:T(8,128)(2,1)S(1)}, bf16[2,128,512]{2,1,0:T(8,128)(2,1)S(1)}, u32[]{:S(2)}, u32[]{:S(2)}) collective-permute-start(bf16[2,128,512]{2,1,0:T(8,128)(2,1)S(1)} %get-tuple-element.27), channel_id=1, source_target_pairs={{0,1},{1,2},{2,3},{3,0},{4,5},{5,6},{6,7},{7,4},{8,9},{9,10},{10,1... | collective-permute-start | bytes 786440 | tf_op jit(solution)/shard_map/ppermute | solution.py:344
  66.8 2.2 %collective-permute-start.17 = (bf16[2,128,512]{2,1,0:T(8,128)(2,1)S(1)}, bf16[2,128,512]{2,1,0:T(8,128)(2,1)S(1)}, u32[]{:S(2)}, u32[]{:S(2)}) collective-permute-start(bf16[2,128,512]{2,1,0:T(8,128)(2,1)S(1)} %get-tuple-element.29), channel_id=1, source_target_pairs={{0,7},{1,4},{2,5},{3,6},{4,3},{5,0},{6,1},{7,2},{8,15},{9,12},{10,... | collective-permute-start | bytes 786440 | tf_op jit(solution)/shard_map/ppermute | solution.py:344
  68.9 2.2 %collective-permute-start.18 = (bf16[2,128,512]{2,1,0:T(8,128)(2,1)S(1)}, bf16[2,128,512]{2,1,0:T(8,128)(2,1)S(1)}, u32[]{:S(2)}, u32[]{:S(2)}) collective-permute-start(bf16[2,128,512]{2,1,0:T(8,128)(2,1)S(1)} %get-tuple-element.30), channel_id=1, source_target_pairs={{0,2},{1,3},{2,0},{3,1},{4,6},{5,7},{6,4},{7,5},{8,10},{9,11},{10,... | collective-permute-start | bytes 786440 | tf_op jit(solution)/shard_map/ppermute | solution.py:344
  71.2 2.9 %collective-permute-done.20.refs_2_ = bf16[2,128,512]{2,1,0:T(8,128)(2,1)S(1)} collective-permute-done((bf16[2,128,512]{2,1,0:T(8,128)(2,1)S(1)}, bf16[2,128,512]{2,1,0:T(8,128)(2,1)S(1)}, u32[]{:S(2)}, u32[]{:S(2)}) %collective-permute-start.20) | collective-permute-done | bytes 262176 | tf_op jit(solution)/shard_map/ppermute | solution.py:344
  74.1 1.3 %collective-permute-start.19 = (bf16[2,128,512]{2,1,0:T(8,128)(2,1)S(1)}, bf16[2,128,512]{2,1,0:T(8,128)(2,1)S(1)}, u32[]{:S(2)}, u32[]{:S(2)}) collective-permute-start(bf16[2,128,512]{2,1,0:T(8,128)(2,1)S(1)} %get-tuple-element.31), channel_id=1, source_target_pairs={{0,4},{1,5},{2,6},{3,7},{4,0},{5,1},{6,2},{7,3},{8,12},{9,13},{10,... | collective-permute-start | bytes 786440 | tf_op jit(solution)/shard_map/ppermute | solution.py:344
  75.4 4.3 %collective-permute-done.21.refs_3_ = bf16[2,128,512]{2,1,0:T(8,128)(2,1)S(1)} collective-permute-done((bf16[2,128,512]{2,1,0:T(8,128)(2,1)S(1)}, bf16[2,128,512]{2,1,0:T(8,128)(2,1)S(1)}, u32[]{:S(2)}, u32[]{:S(2)}) %collective-permute-start.21) | collective-permute-done | bytes 262176 | tf_op jit(solution)/shard_map/ppermute | solution.py:344
  79.8 0.5 collective-permute-start.16
  80.3 1.7 %store.3.refs_4_ = f32[2,8,128,512]{3,2,1,0:T(8,128)} custom-call(s32[3]{0:T(128)S(1)} %pad_add_fusion.refs_0_, bf16[2,128,512]{2,1,0:T(8,128)(2,1)S(1)} %get-tuple-element.32.refs_1_, bf16[2,128,512]{2,1,0:T(8,128)(2,1)S(1)} %collective-permute-done.20.refs_2_, bf16[2,128,512]{2,1,0:T(8,128)(2,1)S(1)} %collective-permute-done.21.refs_3_), custom_call_target="tpu_custom_call" | custom-call | tf_op jit(solution)/shard_map/store/pallas_call | solution.py:348
  82.0 0.4 collective-permute-done.17.refs_1_
  82.5 4.8 %collective-permute-done.18.refs_2_ = bf16[2,128,512]{2,1,0:T(8,128)(2,1)S(1)} collective-permute-done((bf16[2,128,512]{2,1,0:T(8,128)(2,1)S(1)}, bf16[2,128,512]{2,1,0:T(8,128)(2,1)S(1)}, u32[]{:S(2)}, u32[]{:S(2)}) %collective-permute-start.18) | collective-permute-done | bytes 262176 | tf_op jit(solution)/shard_map/ppermute | solution.py:344
  87.3 0.0 collective-permute-done.19.refs_3_
  87.3 1.7 %store.4.refs_3_ = f32[2,8,128,512]{3,2,1,0:T(8,128)} custom-call(s32[3]{0:T(128)S(1)} %pad_add_fusion.refs_0_, bf16[2,128,512]{2,1,0:T(8,128)(2,1)S(1)} %collective-permute-done.17.refs_1_, bf16[2,128,512]{2,1,0:T(8,128)(2,1)S(1)} %collective-permute-done.18.refs_2_, ...), custom_call_target="tpu_custom_call", output_to_operand_aliasing={{}: (4, {})} | custom-call | tf_op jit(solution)/shard_map/store/pallas_call | solution.py:348
  89.1 0.0 collective-permute-done.15.refs_1_
  89.1 0.0 collective-permute-done.16.refs_2_
  89.1 1.6 %store.5 = f32[2,8,128,512]{3,2,1,0:T(8,128)} custom-call(s32[3]{0:T(128)S(1)} %pad_add_fusion.refs_0_, bf16[2,128,512]{2,1,0:T(8,128)(2,1)S(1)} %collective-permute-done.15.refs_1_, bf16[2,128,512]{2,1,0:T(8,128)(2,1)S(1)} %collective-permute-done.16.refs_2_, f32[2,8,128,512]{3,2,1,0:T(8,128)} %store.4.refs_3_), custom_call_target="tpu_custom_call", output_to_operand_aliasing={{}: (3, {})} | custom-call | tf_op jit(solution)/shard_map/store/pallas_call | solution.py:348
  (1 shorter events, 0.0 us)
Async XLA Ops:
  0.1 0.7 copy-start
  4.2 8.0 %collective-permute-start = (f32[96,128]{1,0:T(8,128)S(1)}, f32[96,128]{1,0:T(8,128)S(1)}, u32[]{:S(2)}, u32[]{:S(2)}) collective-permute-start(f32[96,128]{1,0:T(8,128)S(1)} %get-tuple-element.24), channel_id=1, source_target_pairs={{0,1},{1,2},{2,3},{4,5},{5,6},{6,7},{8,9},{9,10},{10,11},{12,13},{... | collective-permute-start | bytes 147464 | tf_op jit(solution)/shard_map/ppermute | solution.py:256
  28.7 9.7 %collective-permute-start.1 = (bf16[4,4,32,128]{3,2,1,0:T(8,128)(2,1)S(1)}, bf16[4,4,32,128]{3,2,1,0:T(8,128)(2,1)S(1)}, u32[]{:S(2)}, u32[]{:S(2)}) collective-permute-start(bf16[4,4,32,128]{3,2,1,0:T(8,128)(2,1)S(1)} %bitcast.8), channel_id=1, source_target_pairs={{0,8},{8,16},{16,24},{24,32},{32,40},{40,48},{48,56},{56,0},{1,9},... | collective-permute-start | bytes 393224 | tf_op jit(solution)/shard_map/ppermute | solution.py:297
  30.6 7.9 %collective-permute-start.4 = (bf16[4,4,32,128]{3,2,1,0:T(8,128)(2,1)S(1)}, bf16[4,4,32,128]{3,2,1,0:T(8,128)(2,1)S(1)}, u32[]{:S(2)}, u32[]{:S(2)}) collective-permute-start(bf16[4,4,32,128]{3,2,1,0:T(8,128)(2,1)S(1)} %bitcast.5), channel_id=1, source_target_pairs={{0,56},{8,0},{16,8},{24,16},{32,24},{40,32},{48,40},{56,48},{1,57}... | collective-permute-start | bytes 393224 | tf_op jit(solution)/shard_map/ppermute | solution.py:298
  34.7 7.6 %collective-permute-start.3 = (bf16[4,4,32,128]{3,2,1,0:T(8,128)(2,1)S(1)}, bf16[4,4,32,128]{3,2,1,0:T(8,128)(2,1)S(1)}, u32[]{:S(2)}, u32[]{:S(2)}) collective-permute-start(bf16[4,4,32,128]{3,2,1,0:T(8,128)(2,1)S(1)} %bitcast.9), channel_id=1, source_target_pairs={{0,56},{8,0},{16,8},{24,16},{32,24},{40,32},{48,40},{56,48},{1,57}... | collective-permute-start | bytes 393224 | tf_op jit(solution)/shard_map/ppermute | solution.py:300
  36.6 7.6 %collective-permute-start.2 = (bf16[4,4,32,128]{3,2,1,0:T(8,128)(2,1)S(1)}, bf16[4,4,32,128]{3,2,1,0:T(8,128)(2,1)S(1)}, u32[]{:S(2)}, u32[]{:S(2)}) collective-permute-start(bf16[4,4,32,128]{3,2,1,0:T(8,128)(2,1)S(1)} %bitcast.6), channel_id=1, source_target_pairs={{0,8},{8,16},{16,24},{24,32},{32,40},{40,48},{48,56},{56,0},{1,9},... | collective-permute-start | bytes 393224 | tf_op jit(solution)/shard_map/ppermute | solution.py:299
  38.4 7.2 %collective-permute-start.5 = (bf16[4,4,32,128]{3,2,1,0:T(8,128)(2,1)S(1)}, bf16[4,4,32,128]{3,2,1,0:T(8,128)(2,1)S(1)}, u32[]{:S(2)}, u32[]{:S(2)}) collective-permute-start(bf16[4,4,32,128]{3,2,1,0:T(8,128)(2,1)S(1)} %collective-permute-done.1.refs_3_), channel_id=1, source_target_pairs={{0,8},{8,16},{16,24},{24,32},{32,40},{40,48},{48,56},{56,0},{1,9},... | collective-permute-start | bytes 393224 | tf_op jit(solution)/shard_map/ppermute | solution.py:297
  38.5 7.3 %collective-permute-start.8 = (bf16[4,4,32,128]{3,2,1,0:T(8,128)(2,1)S(1)}, bf16[4,4,32,128]{3,2,1,0:T(8,128)(2,1)S(1)}, u32[]{:S(2)}, u32[]{:S(2)}) collective-permute-start(bf16[4,4,32,128]{3,2,1,0:T(8,128)(2,1)S(1)} %collective-permute-done.4.refs_6_), channel_id=1, source_target_pairs={{0,56},{8,0},{16,8},{24,16},{32,24},{40,32},{48,40},{56,48},{1,57}... | collective-permute-start | bytes 393224 | tf_op jit(solution)/shard_map/ppermute | solution.py:298
  42.2 7.3 %collective-permute-start.7 = (bf16[4,4,32,128]{3,2,1,0:T(8,128)(2,1)S(1)}, bf16[4,4,32,128]{3,2,1,0:T(8,128)(2,1)S(1)}, u32[]{:S(2)}, u32[]{:S(2)}) collective-permute-start(bf16[4,4,32,128]{3,2,1,0:T(8,128)(2,1)S(1)} %collective-permute-done.3.refs_5_), channel_id=1, source_target_pairs={{0,56},{8,0},{16,8},{24,16},{32,24},{40,32},{48,40},{56,48},{1,57}... | collective-permute-start | bytes 393224 | tf_op jit(solution)/shard_map/ppermute | solution.py:300
  44.2 7.0 %collective-permute-start.6 = (bf16[4,4,32,128]{3,2,1,0:T(8,128)(2,1)S(1)}, bf16[4,4,32,128]{3,2,1,0:T(8,128)(2,1)S(1)}, u32[]{:S(2)}, u32[]{:S(2)}) collective-permute-start(bf16[4,4,32,128]{3,2,1,0:T(8,128)(2,1)S(1)} %collective-permute-done.2.refs_4_), channel_id=1, source_target_pairs={{0,8},{8,16},{16,24},{24,32},{32,40},{40,48},{48,56},{56,0},{1,9},... | collective-permute-start | bytes 393224 | tf_op jit(solution)/shard_map/ppermute | solution.py:299
  45.6 7.0 %collective-permute-start.9 = (bf16[4,4,32,128]{3,2,1,0:T(8,128)(2,1)S(1)}, bf16[4,4,32,128]{3,2,1,0:T(8,128)(2,1)S(1)}, u32[]{:S(2)}, u32[]{:S(2)}) collective-permute-start(bf16[4,4,32,128]{3,2,1,0:T(8,128)(2,1)S(1)} %collective-permute-done.5.refs_7_), channel_id=1, source_target_pairs={{0,8},{8,16},{16,24},{24,32},{32,40},{40,48},{48,56},{56,0},{1,9},... | collective-permute-start | bytes 393224 | tf_op jit(solution)/shard_map/ppermute | solution.py:297
  45.9 7.3 %collective-permute-start.12 = (bf16[4,4,32,128]{3,2,1,0:T(8,128)(2,1)S(1)}, bf16[4,4,32,128]{3,2,1,0:T(8,128)(2,1)S(1)}, u32[]{:S(2)}, u32[]{:S(2)}) collective-permute-start(bf16[4,4,32,128]{3,2,1,0:T(8,128)(2,1)S(1)} %collective-permute-done.8.refs_10_), channel_id=1, source_target_pairs={{0,56},{8,0},{16,8},{24,16},{32,24},{40,32},{48,40},{56,48},{1,57}... | collective-permute-start | bytes 393224 | tf_op jit(solution)/shard_map/ppermute | solution.py:298
  49.6 7.3 %collective-permute-start.11 = (bf16[4,4,32,128]{3,2,1,0:T(8,128)(2,1)S(1)}, bf16[4,4,32,128]{3,2,1,0:T(8,128)(2,1)S(1)}, u32[]{:S(2)}, u32[]{:S(2)}) collective-permute-start(bf16[4,4,32,128]{3,2,1,0:T(8,128)(2,1)S(1)} %collective-permute-done.7.refs_9_), channel_id=1, source_target_pairs={{0,56},{8,0},{16,8},{24,16},{32,24},{40,32},{48,40},{56,48},{1,57}... | collective-permute-start | bytes 393224 | tf_op jit(solution)/shard_map/ppermute | solution.py:300
  51.2 6.7 %collective-permute-start.10 = (bf16[4,4,32,128]{3,2,1,0:T(8,128)(2,1)S(1)}, bf16[4,4,32,128]{3,2,1,0:T(8,128)(2,1)S(1)}, u32[]{:S(2)}, u32[]{:S(2)}) collective-permute-start(bf16[4,4,32,128]{3,2,1,0:T(8,128)(2,1)S(1)} %collective-permute-done.6.refs_8_), channel_id=1, source_target_pairs={{0,8},{8,16},{16,24},{24,32},{32,40},{40,48},{48,56},{56,0},{1,9},... | collective-permute-start | bytes 393224 | tf_op jit(solution)/shard_map/ppermute | solution.py:299
  52.6 7.1 %collective-permute-start.13 = (bf16[4,4,32,128]{3,2,1,0:T(8,128)(2,1)S(1)}, bf16[4,4,32,128]{3,2,1,0:T(8,128)(2,1)S(1)}, u32[]{:S(2)}, u32[]{:S(2)}) collective-permute-start(bf16[4,4,32,128]{3,2,1,0:T(8,128)(2,1)S(1)} %collective-permute-done.9.refs_11_), channel_id=1, source_target_pairs={{0,8},{8,16},{16,24},{24,32},{32,40},{40,48},{48,56},{56,0},{1,9},... | collective-permute-start | bytes 393224 | tf_op jit(solution)/shard_map/ppermute | solution.py:305
  53.1 6.6 %collective-permute-start.14 = (bf16[4,4,32,128]{3,2,1,0:T(8,128)(2,1)S(1)}, bf16[4,4,32,128]{3,2,1,0:T(8,128)(2,1)S(1)}, u32[]{:S(2)}, u32[]{:S(2)}) collective-permute-start(bf16[4,4,32,128]{3,2,1,0:T(8,128)(2,1)S(1)} %collective-permute-done.12.refs_14_), channel_id=1, source_target_pairs={{0,56},{8,0},{16,8},{24,16},{32,24},{40,32},{48,40},{56,48},{1,57}... | collective-permute-start | bytes 393224 | tf_op jit(solution)/shard_map/ppermute | solution.py:306
  60.8 13.3 %collective-permute-start.20 = (bf16[2,128,512]{2,1,0:T(8,128)(2,1)S(1)}, bf16[2,128,512]{2,1,0:T(8,128)(2,1)S(1)}, u32[]{:S(2)}, u32[]{:S(2)}) collective-permute-start(bf16[2,128,512]{2,1,0:T(8,128)(2,1)S(1)} %get-tuple-element.33), channel_id=1, source_target_pairs={{0,6},{1,7},{2,4},{3,5},{4,2},{5,3},{6,0},{7,1},{8,14},{9,15},{10,... | collective-permute-start | bytes 786440 | tf_op jit(solution)/shard_map/ppermute | solution.py:344
  62.5 17.3 %collective-permute-start.21 = (bf16[2,128,512]{2,1,0:T(8,128)(2,1)S(1)}, bf16[2,128,512]{2,1,0:T(8,128)(2,1)S(1)}, u32[]{:S(2)}, u32[]{:S(2)}) collective-permute-start(bf16[2,128,512]{2,1,0:T(8,128)(2,1)S(1)} %get-tuple-element.34), channel_id=1, source_target_pairs={{0,5},{1,6},{2,7},{3,4},{4,1},{5,2},{6,3},{7,0},{8,13},{9,14},{10,... | collective-permute-start | bytes 786440 | tf_op jit(solution)/shard_map/ppermute | solution.py:344
  64.9 24.2 %collective-permute-start.15 = (bf16[2,128,512]{2,1,0:T(8,128)(2,1)S(1)}, bf16[2,128,512]{2,1,0:T(8,128)(2,1)S(1)}, u32[]{:S(2)}, u32[]{:S(2)}) collective-permute-start(bf16[2,128,512]{2,1,0:T(8,128)(2,1)S(1)} %get-tuple-element.27), channel_id=1, source_target_pairs={{0,1},{1,2},{2,3},{3,0},{4,5},{5,6},{6,7},{7,4},{8,9},{9,10},{10,1... | collective-permute-start | bytes 786440 | tf_op jit(solution)/shard_map/ppermute | solution.py:344
  66.8 15.7 %collective-permute-start.17 = (bf16[2,128,512]{2,1,0:T(8,128)(2,1)S(1)}, bf16[2,128,512]{2,1,0:T(8,128)(2,1)S(1)}, u32[]{:S(2)}, u32[]{:S(2)}) collective-permute-start(bf16[2,128,512]{2,1,0:T(8,128)(2,1)S(1)} %get-tuple-element.29), channel_id=1, source_target_pairs={{0,7},{1,4},{2,5},{3,6},{4,3},{5,0},{6,1},{7,2},{8,15},{9,12},{10,... | collective-permute-start | bytes 786440 | tf_op jit(solution)/shard_map/ppermute | solution.py:344
  68.9 18.4 %collective-permute-start.18 = (bf16[2,128,512]{2,1,0:T(8,128)(2,1)S(1)}, bf16[2,128,512]{2,1,0:T(8,128)(2,1)S(1)}, u32[]{:S(2)}, u32[]{:S(2)}) collective-permute-start(bf16[2,128,512]{2,1,0:T(8,128)(2,1)S(1)} %get-tuple-element.30), channel_id=1, source_target_pairs={{0,2},{1,3},{2,0},{3,1},{4,6},{5,7},{6,4},{7,5},{8,10},{9,11},{10,... | collective-permute-start | bytes 786440 | tf_op jit(solution)/shard_map/ppermute | solution.py:344
  74.1 13.2 %collective-permute-start.19 = (bf16[2,128,512]{2,1,0:T(8,128)(2,1)S(1)}, bf16[2,128,512]{2,1,0:T(8,128)(2,1)S(1)}, u32[]{:S(2)}, u32[]{:S(2)}) collective-permute-start(bf16[2,128,512]{2,1,0:T(8,128)(2,1)S(1)} %get-tuple-element.31), channel_id=1, source_target_pairs={{0,4},{1,5},{2,6},{3,7},{4,0},{5,1},{6,2},{7,3},{8,12},{9,13},{10,... | collective-permute-start | bytes 786440 | tf_op jit(solution)/shard_map/ppermute | solution.py:344
  79.8 9.3 %collective-permute-start.16 = (bf16[2,128,512]{2,1,0:T(8,128)(2,1)S(1)}, bf16[2,128,512]{2,1,0:T(8,128)(2,1)S(1)}, u32[]{:S(2)}, u32[]{:S(2)}) collective-permute-start(bf16[2,128,512]{2,1,0:T(8,128)(2,1)S(1)} %get-tuple-element.28), channel_id=1, source_target_pairs={{0,3},{1,0},{2,1},{3,2},{4,7},{5,4},{6,5},{7,6},{8,11},{9,8},{10,9... | collective-permute-start | bytes 786440 | tf_op jit(solution)/shard_map/ppermute | solution.py:344
